TPU v7x, 32 devices: a whole 2x2x4 slice. The times are simulated.
32 devices in a mesh: tx: 4 (over y, core), ty: 8 (over z, x).
Axes of the slice: x: 2, y: 2, z: 4, core: 2. Of those that a mesh axis runs over, the one named last changes fastest.
Arguments:
- increment: float32 [13, 2, 256, 512], P(None, None, 'ty', 'tx'), may hold values from -6 to 6
- blocks: bfloat16 [13, 13, 2, 256, 512], P(None, None, None, 'ty', 'tx'), may hold values from -1.75 to 1.75
- face_weights: float32 [3, 2, 256, 512], P(None, None, 'ty', 'tx'), may hold values from 0.25 to 2
- connected: int32 [3, 2, 256, 512], P(None, None, 'ty', 'tx'), may hold values 0 or 1
- overland_decay: float32 [13, 512, 256], P(None, 'tx', 'ty'), may hold values from 0.4 to 1
- river_cell: int32 [4, 8, 256], P('tx', 'ty'), may hold values from 0 to 4095
- river_reach: int32 [4, 8, 256], P('tx', 'ty'), may hold values from 0 to 255
- river_count: int32 [4, 8], P('tx', 'ty'), may hold values from 64 to 256, as said below
- inflow: float32 [4, 8, 256], P('tx', 'ty'), may hold values from -6 to 6
- outflow: float32 [4, 8, 256], P('tx', 'ty'), may hold values from -3 to 3
- storage: float32 [8, 256], P('ty', 'tx'), may hold values from 1 to 8
Outputs:
- jacobian_product: float32 [13, 2, 256, 512], P(None, None, 'ty', 'tx')
Inputs may be any that keep to these rules, and one draw needn't show every extreme that they name: Each device's live river slots are its first river_count slots; some device fills all 256.
All inputs are finite; a program needn't handle non-finite values. No bound on the sum of `connected` on one device may be relied on, other than what follows from the above.
Results may differ from a plain program's by a relative error of at most 0.0003.
Values sent between devices are 32-bit elements; how exact they have to be, the bound alone decides.
No kernel may reach another device: no remote copies, remote signals or barrier semaphores. Data moves between devices by JAX's collectives and lax.ppermute only.
A program may use at most 128 MiB of HBM per device.

v0:
```python
import functools
import jax
import jax.numpy as jnp
from jax import lax
from jax.experimental import pallas as pl
from jax.experimental.pallas import tpu as pltpu
from jax.sharding import PartitionSpec as P

F32 = jnp.float32
BF16 = jnp.bfloat16
LANES = 128


def log2(n):
    return n.bit_length() - 1


def bit_of(axis, k):
    return (lax.axis_index(axis) >> k) & 1


def split3(x):
    hi = x.astype(BF16).astype(F32)
    rest = x - hi
    mid = rest.astype(BF16).astype(F32)
    return hi, mid, rest - mid


def stack3(row, height):
    hi, mid, lo = split3(row)
    at = lax.broadcasted_iota(jnp.int32, (height, row.shape[1]), 0)
    zero = jnp.zeros((height, row.shape[1]), F32)
    out = jnp.where(at == 0, hi, jnp.where(at == 1, mid, jnp.where(at == 2, lo, zero)))
    return out.astype(BF16)


def hot(index_row, size, start=0):
    at = lax.broadcasted_iota(jnp.int32, (size, index_row.shape[1]), 0) + start
    return at == index_row


def fetch(pairs, sems):
    copies = [pltpu.make_async_copy(src, dst, sems.at[i]) for i, (src, dst) in enumerate(pairs)]
    for copy in copies:
        copy.start()
    return copies


def summary_kernel(inc_hbm, dec_hbm, fw_hbm, con_hbm, ysend_ref, inc_ref, dec_ref, fw_ref, con_ref, sems):
    unknowns, layers, rows, cols = inc_ref.shape
    tile = pl.ds(rows - fw_ref.shape[1], fw_ref.shape[1])
    copies = fetch(
        [
            (inc_hbm, inc_ref), (dec_hbm, dec_ref), (fw_hbm.at[1, :, tile, :], fw_ref),
            (con_hbm.at[1, :, tile, :], con_ref),
        ],
        sems,
    )
    ysend_ref[...] = jnp.zeros(ysend_ref.shape, F32)
    copies[0].wait()
    for layer in range(layers):
        ysend_ref[2 + layer, 0:unknowns] = inc_ref[:, layer, 0, :]
        ysend_ref[2 + layers + layer, 0:unknowns] = inc_ref[:, layer, rows - 1, :]
    copies[1].wait()
    product = dec_ref[:, 0, :]
    value = inc_ref[:, 0, 0, :]
    for y in range(1, rows):
        decay = dec_ref[:, y, :]
        product = product * decay
        value = value * decay + inc_ref[:, 0, y, :]
    ysend_ref[0, 0:unknowns] = product
    ysend_ref[1, 0:unknowns] = value
    copies[2].wait()
    copies[3].wait()
    for layer in range(layers):
        face = fw_ref[layer, -1:, :] * con_ref[layer, -1:, :].astype(F32)
        ysend_ref[2 + layers + layer, unknowns:unknowns + 1] = face


def river_rows(xsend_ref, rows, at, value):
    for c in range(value.shape[1] // LANES):
        xsend_ref[pl.ds(rows + at + c, 1), :] = value[:, c * LANES:(c + 1) * LANES]


def columns_kernel(
    pad, inc_hbm, fw_hbm, con_hbm, cell_hbm, reach_hbm, count_hbm, inflow_hbm, outflow_hbm, storage_hbm,
    xsend_ref, inc_ref, fw_ref, con_ref, cell_ref, reach_ref, count_ref, inflow_ref, outflow_ref, storage_ref, sems,
):
    copies = fetch(
        [
            (cell_hbm, cell_ref), (reach_hbm, reach_ref), (count_hbm, count_ref), (inflow_hbm, inflow_ref),
            (outflow_hbm, outflow_ref), (storage_hbm, storage_ref), (inc_hbm, inc_ref),
            (fw_hbm.at[0], fw_ref), (con_hbm.at[0], con_ref),
        ],
        sems,
    )
    unknowns, layers, rows, cols = inc_ref.shape
    xsend_ref[rows:, :] = jnp.zeros((xsend_ref.shape[0] - rows, LANES), F32)
    for copy in copies:
        copy.wait()
    cells = cell_ref[0]
    reaches = reach_ref[0]
    slots = cells.shape[1]
    wide = slots // LANES
    shift = log2(cols)
    parts = jnp.concatenate(split3(inc_ref[0, 0]), 0).astype(BF16)
    y_hot = hot(cells >> shift, rows).astype(F32)
    y_hot3 = jnp.concatenate([y_hot, y_hot, y_hot], 0).astype(BF16)
    picked = lax.dot_general(parts, y_hot3, (((0,), (0,)), ((), ())), preferred_element_type=F32)
    values = jnp.sum(jnp.where(hot(cells & (cols - 1), cols), picked, 0.0), 0, keepdims=True)
    live = lax.broadcasted_iota(jnp.int32, (1, slots), 1) < count_ref[...]
    terms = stack3(jnp.where(live, inflow_ref[0] * values, 0.0), 16)
    river_rows(xsend_ref, rows, 2 * pad, cells.astype(F32))
    river_rows(xsend_ref, rows, 2 * pad + wide, reaches.astype(F32))
    river_rows(xsend_ref, rows, 2 * pad + 2 * wide, jnp.where(live, outflow_ref[0], 0.0))
    reach_local = storage_ref.shape[1]
    x_index = lax.axis_index("tx")
    stored = jnp.concatenate([storage_ref[...]] * (LANES // reach_local), 1)
    owner = lax.broadcasted_iota(jnp.int32, (1, LANES), 1)
    for c in range(reach_local * lax.axis_size("tx") // LANES):
        r_hot = hot(reaches, LANES, c * LANES).astype(F32).astype(BF16)
        total = lax.dot_general(terms, r_hot, (((1,), (1,)), ((), ())), preferred_element_type=F32)
        xsend_ref[pl.ds(rows + c, 1), :] = jnp.sum(total, 0, keepdims=True)
        xsend_ref[pl.ds(rows + pad + c, 1), :] = jnp.where(
            (owner + c * LANES) // reach_local == x_index, stored, 0.0
        )
    pair = lax.broadcasted_iota(jnp.int32, (rows, cols), 1) >> 1
    packed = jnp.zeros((rows, cols), F32)
    for p in range(unknowns * layers + layers):
        if p < unknowns * layers:
            plane = inc_ref[p // layers, p % layers]
        else:
            layer = p - unknowns * layers
            plane = fw_ref[layer] * con_ref[layer].astype(F32)
        packed = jnp.where(pair == p, pltpu.roll(plane, 2 * p + 1, 1), packed)
    xsend_ref[0:rows, :] = packed


def prefix_step(k, received, prior):
    upper = bit_of("ty", k) == 1
    if prior is None:
        return jnp.where(upper, received[0], 1.0), jnp.where(upper, received[1], 0.0)
    product = jnp.where(upper, prior[0] * received[0], prior[0])
    value = jnp.where(upper, prior[0] * received[1] + prior[1], prior[1])
    return product, value


def between_kernel(k, layers, sums, sent_ref, got_ref, *refs):
    refs = list(refs)
    prior_ref = refs.pop(0) if k > 0 else None
    if sums is not None:
        xsent_ref, xgot_ref = refs[:2]
        xsend_ref = refs.pop()
        start, stop = sums
        xsend_ref[...] = xsent_ref[...]
        xsend_ref[start:stop, :] = xsent_ref[start:stop, :] + xgot_ref[start:stop, :]
    send_ref, next_ref = refs[-2:]
    upper = bit_of("ty", k) == 1
    product, value = prefix_step(k, got_ref, prior_ref)
    next_ref[0] = product
    next_ref[1] = value
    own_a, own_b, got_a, got_b = sent_ref[0], sent_ref[1], got_ref[0], got_ref[1]
    low_b = jnp.where(upper, got_b, own_b)
    up_a = jnp.where(upper, own_a, got_a)
    up_b = jnp.where(upper, own_b, got_b)
    send_ref[0] = own_a * got_a
    send_ref[1] = up_a * low_b + up_b
    for layer in range(layers):
        passed = got_ref[2 + layer]
        if k == 0:
            passed = jnp.where(upper, passed, got_ref[2 + layers + layer])
        send_ref[2 + layer] = passed


def beside_x(received, rows):
    index = lax.axis_index("tx")
    below = jnp.zeros((rows, LANES), F32)
    above = below
    for k, buffer in enumerate(received):
        low = (1 << k) - 1
        full = (2 << k) - 1
        above = jnp.where((index & full) == low, buffer[0:rows, :], above)
        below = jnp.where((index & full) == low + 1, buffer[0:rows, :], below)
    return below, above


def local_kernel(x_rounds, pad, reach_rows, slots, *refs):
    blocks_hbm, inc_hbm, dec_hbm, fw_hbm, con_hbm, sent_ref = refs[:6]
    received = refs[6:6 + x_rounds]
    inc_ref, dec_ref, fw_ref, con_ref, blocks_ref, value_ref, product_ref, sems = refs[-8:]
    unknowns, layers, rows, cols = inc_ref.shape
    out_refs = refs[6 + x_rounds:6 + x_rounds + unknowns]
    grown_refs = refs[6 + x_rounds + unknowns:6 + x_rounds + 2 * unknowns]
    copies = fetch(
        [(inc_hbm, inc_ref), (dec_hbm, dec_ref), (fw_hbm, fw_ref), (con_hbm, con_ref)]
        + [(blocks_hbm.at[i], blocks_ref.at[i]) for i in range(unknowns)],
        sems,
    )
    lane = lax.broadcasted_iota(jnp.int32, (rows, cols), 1)
    row = lax.broadcasted_iota(jnp.int32, (rows, cols), 0)
    wide = slots // LANES

    def slot_row(at):
        start = rows + 2 * pad + at * wide
        return jnp.concatenate([sent_ref[start + c:start + c + 1, :] for c in range(wide)], 1)

    cells = slot_row(0).astype(jnp.int32)
    reaches = slot_row(1).astype(jnp.int32)
    totals = sent_ref[rows:rows + pad, :] + received[-1][rows:rows + pad, :]
    storage = sent_ref[rows + pad:rows + 2 * pad, :] + received[-1][rows + pad:rows + 2 * pad, :]
    shift = log2(cols)
    picked = jnp.zeros((16, slots), F32)
    for c in range(reach_rows):
        section = stack3(totals[c:c + 1] / storage[c:c + 1], 16)
        r_hot = hot(reaches, LANES, c * LANES).astype(F32).astype(BF16)
        picked = picked + lax.dot_general(section, r_hot, (((1,), (0,)), ((), ())), preferred_element_type=F32)
    back = slot_row(2) * jnp.sum(picked, 0, keepdims=True)
    y_hot = hot(cells >> shift, rows)
    spread = jnp.concatenate([jnp.where(y_hot, part, 0.0) for part in split3(back)], 0).astype(BF16)
    x_hot = hot(cells & (cols - 1), cols).astype(F32).astype(BF16)
    added = lax.dot_general(spread, x_hot, (((1,), (1,)), ((), ())), preferred_element_type=F32)
    river = added[0:rows] + added[rows:2 * rows] + added[2 * rows:3 * rows]
    copies[0].wait()
    copies[1].wait()
    product = 0.1 * dec_ref[:, 0, :]
    value = 0.1 * inc_ref[:, 0, 0, :]
    product_ref[:, 0, :] = product
    value_ref[:, 0, :] = value
    for y in range(1, rows):
        decay = dec_ref[:, y, :]
        product = product * decay
        value = value * decay + 0.1 * inc_ref[:, 0, y, :]
        product_ref[:, y, :] = product
        value_ref[:, y, :] = value
    copies[2].wait()
    copies[3].wait()
    left, right = beside_x(received, rows)
    rim = jnp.where(lane & 1 == 0, pltpu.roll(right, cols - 1, 1), pltpu.roll(left, 1, 1))
    planes = unknowns * layers
    for u in range(unknowns):
        grown_refs[u][...] = product_ref[u]
        copies[4 + u].wait()
        for layer in range(layers):
            face_x = fw_ref[0, layer] * con_ref[0, layer].astype(F32)
            face_y = jnp.where(row == rows - 1, 0.0, fw_ref[1, layer] * con_ref[1, layer].astype(F32))
            face_z = fw_ref[2, layer] * con_ref[2, layer].astype(F32)
            face_left = pltpu.roll(rim, (cols - 1 - 2 * (planes + layer)) % cols, 1)
            here = inc_ref[u, layer]
            p = u * layers + layer
            beside = pltpu.roll(rim, cols - 1 - 2 * p, 1)
            flow_x = face_x * (here - jnp.where(lane == cols - 1, beside, pltpu.roll(here, cols - 1, 1)))
            from_left = jnp.where(lane == 0, face_left * (beside - here), pltpu.roll(flow_x, 1, 1))
            flow_y = face_y * (here - pltpu.roll(here, rows - 1, 0))
            total = flow_x - from_left + (flow_y - pltpu.roll(flow_y, 1, 0))
            if layer + 1 < layers:
                total = total + face_z * (here - inc_ref[u, layer + 1])
            else:
                total = total + face_z * here
            if layer > 0:
                face_above = fw_ref[2, layer - 1] * con_ref[2, layer - 1].astype(F32)
                total = total + face_above * (here - inc_ref[u, layer - 1])
            else:
                total = total + value_ref[u]
                if u == 0:
                    total = total + river
            for j in range(unknowns):
                total = total + blocks_ref[u, j, layer].astype(F32) * inc_ref[j, layer]
            out_refs[u][layer] = total


def final_kernel(unknowns, y_rounds, *refs):
    part_refs = refs[:unknowns]
    grown_refs = refs[unknowns:2 * unknowns]
    own_ref = refs[2 * unknowns]
    got = refs[2 * unknowns + 1:2 * unknowns + 1 + y_rounds]
    prior_ref, out_ref = refs[-2:]
    layers, rows, cols = part_refs[0].shape
    _, carry = prefix_step(y_rounds - 1, got[-1], prior_ref)
    index = lax.axis_index("ty")
    odd = (index & 1) == 1
    at = lax.broadcasted_iota(jnp.int32, (8, cols), 0)
    starts = []
    ends = []
    for layer in range(layers):
        passed_up = jnp.zeros(carry.shape, F32)
        passed_down = passed_up
        for k in range(1, y_rounds):
            full = (2 << k) - 1
            passed_up = jnp.where((index & full) == (1 << k), got[k][2 + layer], passed_up)
            passed_down = jnp.where((index & full) == (1 << k) - 1, got[k][2 + layer], passed_down)
        below = jnp.where(odd, got[0][2 + layers + layer], passed_up)
        above = jnp.where(odd, passed_down, got[0][2 + layer])
        low_face = below[unknowns:unknowns + 1]
        top_face = own_ref[2 + layers + layer, unknowns:unknowns + 1]
        starts.append(low_face * (own_ref[2 + layer] - below))
        ends.append(top_face * (own_ref[2 + layers + layer] - above))
    for u in range(unknowns):
        for layer in range(layers):
            total = part_refs[u][layer]
            if layer == 0:
                total = total + grown_refs[u][...] * carry[u:u + 1]
            head = total[0:8] + jnp.where(at == 0, starts[layer][u:u + 1], 0.0)
            foot = total[rows - 8:rows] + jnp.where(at == 7, ends[layer][u:u + 1], 0.0)
            out_ref[u, layer, 0:8, :] = head
            out_ref[u, layer, 8:rows - 8, :] = total[8:rows - 8]
            out_ref[u, layer, rows - 8:rows, :] = foot


def call(kernel, outs, args, far=0, scratch=(), grant=32 * 1024, cost=0):
    vmem = pl.BlockSpec(memory_space=pltpu.VMEM)
    hbm = pl.BlockSpec(memory_space=pltpu.HBM)
    return pl.pallas_call(
        kernel,
        out_shape=[jax.ShapeDtypeStruct(o.shape, o.dtype) for o in outs],
        in_specs=[hbm] * far + [vmem] * (len(args) - far),
        out_specs=[vmem] * len(outs),
        scratch_shapes=list(scratch),
        compiler_params=pltpu.CompilerParams(vmem_limit_bytes=grant * 1024),
        cost_estimate=pl.CostEstimate(flops=0, bytes_accessed=cost, transcendentals=0),
    )(*args)


def f32(*shape):
    return jax.ShapeDtypeStruct(shape, F32)


def like(a, *shape):
    return pltpu.VMEM(shape or a.shape, a.dtype)


SUMMARY_GRANT = 55160
COLUMNS_GRANT = 56000
LOCAL_GRANT = 54440
LOCAL_COST = 0
COLUMNS_COST = 0


def body(
    increment,
    blocks,
    face_weights,
    connected,
    overland_decay,
    river_cell,
    river_reach,
    river_count,
    inflow,
    outflow,
    storage,
):
    unknowns, layers, rows, cols = increment.shape
    x_size = lax.axis_size("tx")
    y_size = lax.axis_size("ty")
    x_rounds = log2(x_size)
    y_rounds = log2(y_size)
    slots = river_cell.shape[2]
    decay = jnp.swapaxes(overland_decay, 1, 2)
    reach_rows = storage.shape[1] * x_size // LANES
    pad = -(-reach_rows // 8) * 8
    tall = -(-(unknowns + 1) // 8) * 8
    edge = (layers, 8, cols)
    (y_first,) = call(
        summary_kernel,
        [f32(2 + 2 * layers, tall, cols)],
        [increment, decay, face_weights, connected],
        far=4,
        scratch=[
            like(increment), like(decay), like(face_weights, *edge), like(connected, *edge),
            pltpu.SemaphoreType.DMA((4,)),
        ],
        grant=SUMMARY_GRANT,
    )
    args = [
        increment, face_weights, connected, river_cell, river_reach, river_count, inflow, outflow, storage,
    ]
    (x_send,) = call(
        functools.partial(columns_kernel, pad),
        [f32(rows + 2 * pad + -(-3 * slots // LANES // 8) * 8, cols)],
        args,
        far=len(args),
        scratch=[like(increment)]
        + [like(a, layers, rows, cols) for a in args[1:3]]
        + [like(a) for a in args[3:]]
        + [pltpu.SemaphoreType.DMA((len(args),))],
        grant=COLUMNS_GRANT,
        cost=COLUMNS_COST,
    )
    y_send = y_first
    y_got = []
    x_got = []
    prior = None
    for k in range(max(x_rounds, y_rounds)):
        more_x = k + 1 < x_rounds
        more_y = k + 1 < y_rounds
        if k < y_rounds:
            y_got.append(lax.ppermute(y_send, "ty", [(i, i ^ (1 << k)) for i in range(y_size)]))
        if k < x_rounds:
            x_got.append(lax.ppermute(x_send, "tx", [(i, i ^ ((2 << k) - 1)) for i in range(x_size)]))
        if more_x or more_y:
            made = call(
                functools.partial(between_kernel, k, layers, (rows, rows + 2 * pad) if more_x else None),
                [f32(2 + layers, tall, cols), f32(2, tall, cols)] + ([x_send] if more_x else []),
                [y_send, y_got[-1]]
                + ([prior] if k > 0 else [])
                + ([x_send] if more_x else [])
                + (x_got[-1:] if k < x_rounds else []),
            )
            y_send, prior = made[:2]
            if more_x:
                x_send = made[2]
    local = call(
        functools.partial(local_kernel, x_rounds, pad, reach_rows, slots),
        [f32(layers, rows, cols)] * unknowns + [f32(rows, cols)] * unknowns,
        [blocks, increment, decay, face_weights, connected, x_send, *x_got],
        far=5,
        scratch=[
            like(increment), like(decay), like(face_weights), like(connected), like(blocks), like(decay), like(decay),
            pltpu.SemaphoreType.DMA((4 + unknowns,)),
        ],
        grant=LOCAL_GRANT,
        cost=LOCAL_COST,
    )
    (total,) = call(
        functools.partial(final_kernel, unknowns, y_rounds),
        [increment],
        [*local, y_first, *y_got, prior],
    )
    return total


def solution(mesh):
    in_specs = (
        P(None, None, "ty", "tx"),
        P(None, None, None, "ty", "tx"),
        P(None, None, "ty", "tx"),
        P(None, None, "ty", "tx"),
        P(None, "tx", "ty"),
        P("tx", "ty", None),
        P("tx", "ty", None),
        P("tx", "ty"),
        P("tx", "ty", None),
        P("tx", "ty", None),
        P("ty", "tx"),
    )
    out_specs = P(None, None, "ty", "tx")
    return jax.shard_map(body, mesh=mesh, in_specs=in_specs, out_specs=out_specs, check_vma=False)
```

profile of v0, /device:TPU:0, one launch (start us, length us, event | category | flops | bytes accessed | tf_op | source)
XLA Modules:
  0.0 22.2 jit_solution(14444166555121334232)
XLA Ops:
  0.0 1.3 %shard_map.109.sent_ref.refs_26_ = f32[6,16,128]{2,1,0:T(8,128)S(1)} custom-call(f32[13,2,32,128]{3,2,1,0:T(8,128)} %refs_1_.1, f32[13,32,128]{2,1,0:T(8,128)} %bitcast.1, f32[3,2,32,128]{3,2,1,0:T(8,128)} %refs_3_.1, s32[3,2,32,128]{3,2,1,0:T(8,128)} %refs_4_.1), custom_call_target="tpu_custom_call" | custom-call | tf_op jit(solution)/shard_map/pallas_call | solution.py:312
  1.3 3.0 %collective-permute-start = (f32[6,16,128]{2,1,0:T(8,128)S(1)}, f32[6,16,128]{2,1,0:T(8,128)S(1)}, u32[]{:S(2)}, u32[]{:S(2)}) collective-permute-start(f32[6,16,128]{2,1,0:T(8,128)S(1)} %shard_map.109.sent_ref.refs_26_), channel_id=1, source_target_pairs={{0,1},{1,0},{2,3},{3,2},{4,5},{5,4},{6,7},{7,6},{8,9},{9,8},{10,11... | collective-permute-start | bytes 147464 | tf_op jit(solution)/shard_map/ppermute | solution.py:396
  4.9 2.1 %shard_map.110.refs_0_ = f32[56,128]{1,0:T(8,128)} custom-call(f32[13,2,32,128]{3,2,1,0:T(8,128)} %refs_1_.1, f32[3,2,32,128]{3,2,1,0:T(8,128)} %refs_3_.1, s32[3,2,32,128]{3,2,1,0:T(8,128)} %refs_4_.1, s32[1,1,256]{2,1,0:T(1,128)} %cell_hbm.1, s32[1,1,256]{2,1,0:T(1,128)} %reach_hbm.1, s32[1,1]{1,0:T(1,128)S(6)} %copy.12.count_hbm, ...), custom_call_target="tpu_custom_call" | custom-call | tf_op jit(solution)/shard_map/pallas_call | solution.py:312
  7.1 0.1 collective-permute-start.1
  7.2 1.4 %collective-permute-done.1.refs_1_.refs_6_ = f32[56,128]{1,0:T(8,128)S(1)} collective-permute-done((f32[56,128]{1,0:T(8,128)}, f32[56,128]{1,0:T(8,128)S(1)}, u32[]{:S(2)}, u32[]{:S(2)}) %collective-permute-start.1) | collective-permute-done | bytes 28704 | tf_op jit(solution)/shard_map/ppermute | solution.py:398
  8.6 0.0 collective-permute-done.got_ref.refs_27_
  8.6 0.0 copy-start
  8.6 0.7 %copy-done = f32[56,128]{1,0:T(8,128)S(1)} copy-done((f32[56,128]{1,0:T(8,128)S(1)}, f32[56,128]{1,0:T(8,128)}, u32[]{:S(2)}) %copy-start) | copy-done | bytes 28696
  9.3 1.6 %collective-permute-start.3 = (f32[4,16,128]{2,1,0:T(8,128)S(1)}, f32[4,16,128]{2,1,0:T(8,128)S(1)}, u32[]{:S(2)}, u32[]{:S(2)}) collective-permute-start(f32[4,16,128]{2,1,0:T(8,128)S(1)} %get-tuple-element.63.sent_ref), channel_id=1, source_target_pairs={{0,2},{1,3},{2,0},{3,1},{4,6},{5,7},{6,4},{7,5},{8,10},{9,11},{10,... | collective-permute-start | bytes 98312 | tf_op jit(solution)/shard_map/ppermute | solution.py:396
  11.0 1.0 %collective-permute-start.2 = (f32[56,128]{1,0:T(8,128)S(1)}, f32[56,128]{1,0:T(8,128)S(1)}, u32[]{:S(2)}, u32[]{:S(2)}) collective-permute-start(f32[56,128]{1,0:T(8,128)S(1)} %get-tuple-element.36.refs_5_), channel_id=1, source_target_pairs={{0,24},{8,16},{16,8},{24,0},{1,25},{9,17},{17,9},{25,1},{2,26},{10... | collective-permute-start | bytes 86024 | tf_op jit(solution)/shard_map/ppermute | solution.py:398
  12.0 2.5 %collective-permute-done.2.refs_7_.refs_1_ = f32[56,128]{1,0:T(8,128)S(1)} collective-permute-done((f32[56,128]{1,0:T(8,128)S(1)}, f32[56,128]{1,0:T(8,128)S(1)}, u32[]{:S(2)}, u32[]{:S(2)}) %collective-permute-start.2) | collective-permute-done | bytes 28704 | tf_op jit(solution)/shard_map/ppermute | solution.py:398
  14.5 0.0 collective-permute-done.3.got_ref.refs_28_
  14.5 2.7 %collective-permute-start.4 = (f32[4,16,128]{2,1,0:T(8,128)S(1)}, f32[4,16,128]{2,1,0:T(8,128)S(1)}, u32[]{:S(2)}, u32[]{:S(2)}) collective-permute-start(f32[4,16,128]{2,1,0:T(8,128)S(1)} %get-tuple-element.65), channel_id=1, source_target_pairs={{0,4},{1,5},{2,6},{3,7},{4,0},{5,1},{6,2},{7,3},{8,12},{9,13},{10,... | collective-permute-start | bytes 98312 | tf_op jit(solution)/shard_map/ppermute | solution.py:396
  17.2 4.1 %shard_map.112 = (f32[2,32,128]{2,1,0:T(8,128)S(1)}, f32[2,32,128]{2,1,0:T(8,128)S(1)}, f32[2,32,128]{2,1,0:T(8,128)S(1)}, f32[2,32,128]{2,1,0:T(8,128)S(1)}, f3...) custom-call(bf16[13,13,2,32,128]{4,3,2,1,0:T(8,128)(2,1)} %refs_0_.1, ...), custom_call_target="tpu_custom_call" | custom-call | tf_op jit(solution)/shard_map/pallas_call | solution.py:312
  21.3 0.0 collective-permute-done.4.refs_29_
  21.3 0.9 %shard_map.114 = f32[13,2,32,128]{3,2,1,0:T(8,128)} custom-call(f32[2,32,128]{2,1,0:T(8,128)S(1)} %get-tuple-element.37.refs_0_, f32[2,32,128]{2,1,0:T(8,128)S(1)} %get-tuple-element.38.refs_1_, f32[2,32,128]{2,1,0:T(8,128)S(1)} %get-tuple-element.39.refs_2_, f32[2,32,128]{2,1,0:T(8,128)S(1)} %get-tuple-element.40.refs_3_, ...), custom_call_target="tpu_custom_call" | custom-call | tf_op jit(solution)/shard_map/pallas_call | solution.py:312
  (2 shorter events, 0.0 us)
Async XLA Ops:
  1.3 7.3 %collective-permute-start = (f32[6,16,128]{2,1,0:T(8,128)S(1)}, f32[6,16,128]{2,1,0:T(8,128)S(1)}, u32[]{:S(2)}, u32[]{:S(2)}) collective-permute-start(f32[6,16,128]{2,1,0:T(8,128)S(1)} %shard_map.109.sent_ref.refs_26_), channel_id=1, source_target_pairs={{0,1},{1,0},{2,3},{3,2},{4,5},{5,4},{6,7},{7,6},{8,9},{9,8},{10,11... | collective-permute-start | bytes 147464 | tf_op jit(solution)/shard_map/ppermute | solution.py:396
  7.1 1.5 %collective-permute-start.1 = (f32[56,128]{1,0:T(8,128)}, f32[56,128]{1,0:T(8,128)S(1)}, u32[]{:S(2)}, u32[]{:S(2)}) collective-permute-start(f32[56,128]{1,0:T(8,128)} %shard_map.110.refs_0_), channel_id=1, source_target_pairs={{0,8},{8,0},{16,24},{24,16},{1,9},{9,1},{17,25},{25,17},{2,10},{10... | collective-permute-start | bytes 86024 | tf_op jit(solution)/shard_map/ppermute | solution.py:398
  8.6 0.7 %copy-start = (f32[56,128]{1,0:T(8,128)S(1)}, f32[56,128]{1,0:T(8,128)}, u32[]{:S(2)}) copy-start(f32[56,128]{1,0:T(8,128)} %shard_map.110.refs_0_) | copy-start | bytes 86020
  9.3 5.2 %collective-permute-start.3 = (f32[4,16,128]{2,1,0:T(8,128)S(1)}, f32[4,16,128]{2,1,0:T(8,128)S(1)}, u32[]{:S(2)}, u32[]{:S(2)}) collective-permute-start(f32[4,16,128]{2,1,0:T(8,128)S(1)} %get-tuple-element.63.sent_ref), channel_id=1, source_target_pairs={{0,2},{1,3},{2,0},{3,1},{4,6},{5,7},{6,4},{7,5},{8,10},{9,11},{10,... | collective-permute-start | bytes 98312 | tf_op jit(solution)/shard_map/ppermute | solution.py:396
  11.0 3.5 %collective-permute-start.2 = (f32[56,128]{1,0:T(8,128)S(1)}, f32[56,128]{1,0:T(8,128)S(1)}, u32[]{:S(2)}, u32[]{:S(2)}) collective-permute-start(f32[56,128]{1,0:T(8,128)S(1)} %get-tuple-element.36.refs_5_), channel_id=1, source_target_pairs={{0,24},{8,16},{16,8},{24,0},{1,25},{9,17},{17,9},{25,1},{2,26},{10... | collective-permute-start | bytes 86024 | tf_op jit(solution)/shard_map/ppermute | solution.py:398
  14.5 6.8 %collective-permute-start.4 = (f32[4,16,128]{2,1,0:T(8,128)S(1)}, f32[4,16,128]{2,1,0:T(8,128)S(1)}, u32[]{:S(2)}, u32[]{:S(2)}) collective-permute-start(f32[4,16,128]{2,1,0:T(8,128)S(1)} %get-tuple-element.65), channel_id=1, source_target_pairs={{0,4},{1,5},{2,6},{3,7},{4,0},{5,1},{6,2},{7,3},{8,12},{9,13},{10,... | collective-permute-start | bytes 98312 | tf_op jit(solution)/shard_map/ppermute | solution.py:396
where the time goes:
time: 22.4 us; the launch traced here: 22.2 us
  Pallas kernels  8.43 us (38%)
  starting transfers between devices  8.38 us (37%)
  waiting for transfers between devices  3.93 us (18%)
  local copies, waits for them, and re-layouts  0.75 us (3%)
  between operations  0.71 us (3%)
    pallas_call x6, Pallas kernels, call(): pl.pallas_call(kernel, out_shape=[jax.ShapeDtypeStruct(o.shape, o.dtype)...  8.43 us
    ppermute x3, starting transfers between devices, body(): lax.ppermute(y_send, 'ty', [(i, i ^ 1 << k) for i in range(y_size)])  7.3 us
    ppermute x2, waiting for transfers between devices, body(): lax.ppermute(x_send, 'tx', [(i, i ^ (2 << k) - 1) for i in range(x_size)])  3.92 us
    ppermute x2, starting transfers between devices, body(): lax.ppermute(x_send, 'tx', [(i, i ^ (2 << k) - 1) for i in range(x_size)])  1.08 us
    unnamed x2, local copies, waits for them, and re-layouts  0.75 us
  transfers between devices with their start and end apart: 5, of which 2 were waited for; matrix products, arithmetic and copies ran while one was open for 0% of the time, Pallas kernels for 28%

commit v1 on v0

v1 whole, which is shorter than its diff:
```python
import functools
import jax
import jax.numpy as jnp
from jax import lax
from jax.experimental import pallas as pl
from jax.experimental.pallas import tpu as pltpu
from jax.sharding import PartitionSpec as P

F32 = jnp.float32
BF16 = jnp.bfloat16
LANES = 128


def log2(n):
    return n.bit_length() - 1


def bit_of(axis, k):
    return (lax.axis_index(axis) >> k) & 1


def split3(x):
    hi = x.astype(BF16).astype(F32)
    rest = x - hi
    mid = rest.astype(BF16).astype(F32)
    return hi, mid, rest - mid


def stack3(row, height):
    hi, mid, lo = split3(row)
    at = lax.broadcasted_iota(jnp.int32, (height, row.shape[1]), 0)
    zero = jnp.zeros((height, row.shape[1]), F32)
    out = jnp.where(at == 0, hi, jnp.where(at == 1, mid, jnp.where(at == 2, lo, zero)))
    return out.astype(BF16)


def hot(index_row, size, start=0):
    at = lax.broadcasted_iota(jnp.int32, (size, index_row.shape[1]), 0) + start
    return at == index_row


def fetch(pairs, sems):
    copies = [pltpu.make_async_copy(src, dst, sems.at[i]) for i, (src, dst) in enumerate(pairs)]
    for copy in copies:
        copy.start()
    return copies


def summary_kernel(unknowns, inc_hbm, dec_hbm, fw_hbm, con_hbm, ysend_ref, packed_ref, *refs):
    inc_out = refs[:unknowns]
    face_out = refs[unknowns:-5]
    inc_ref, dec_ref, fw_ref, con_ref, sems = refs[-5:]
    _, layers, rows, cols = inc_ref.shape
    copies = fetch([(inc_hbm, inc_ref), (dec_hbm, dec_ref), (fw_hbm, fw_ref), (con_hbm, con_ref)], sems)
    ysend_ref[...] = jnp.zeros(ysend_ref.shape, F32)
    for copy in copies:
        copy.wait()
    product = dec_ref[:, 0, :]
    value = inc_ref[:, 0, 0, :]
    for y in range(1, rows):
        decay = dec_ref[:, y, :]
        product = product * decay
        value = value * decay + inc_ref[:, 0, y, :]
    pair = lax.broadcasted_iota(jnp.int32, (rows, cols), 1) >> 1
    row = lax.broadcasted_iota(jnp.int32, (rows, cols), 0)
    packed = jnp.zeros((rows, cols), F32)
    planes = unknowns * layers
    for p in range(planes):
        packed = jnp.where(pair == p, pltpu.roll(inc_ref[p // layers, p % layers], 2 * p + 1, 1), packed)
    faces = [[fw_ref[d, l] * con_ref[d, l].astype(F32) for l in range(layers)] for d in range(3)]
    for layer in range(layers):
        p = planes + layer
        packed = jnp.where(pair == p, pltpu.roll(faces[0][layer], 2 * p + 1, 1), packed)
    ysend_ref[0, 0:unknowns] = product
    ysend_ref[1, 0:unknowns] = value
    for layer in range(layers):
        ysend_ref[2 + layer, 0:unknowns] = inc_ref[:, layer, 0, :]
        ysend_ref[2 + layers + layer, 0:unknowns] = inc_ref[:, layer, rows - 1, :]
        ysend_ref[2 + layers + layer, unknowns:unknowns + 1] = faces[1][layer][rows - 1:]
        face_out[layer][...] = faces[0][layer]
        face_out[layers + layer][...] = jnp.where(row == rows - 1, 0.0, faces[1][layer])
        face_out[2 * layers + layer][...] = faces[2][layer]
    packed_ref[...] = packed
    for u in range(unknowns):
        inc_out[u][...] = inc_ref[u]


def river_rows(xsend_ref, rows, at, value):
    for c in range(value.shape[1] // LANES):
        xsend_ref[pl.ds(rows + at + c, 1), :] = value[:, c * LANES:(c + 1) * LANES]


def river_kernel(pad, reach_local, code_ref, outflow_ref, inflow_ref, storage_ref, packed_ref, inc_ref, _, xsend_ref):
    layers, rows, cols = inc_ref.shape
    slots = code_ref.shape[2]
    wide = slots // LANES
    code = code_ref[0].astype(jnp.int32)
    reaches = code >> log2(rows * cols)
    cells = code & (rows * cols - 1)
    xsend_ref[rows:, :] = jnp.zeros((xsend_ref.shape[0] - rows, LANES), F32)
    xsend_ref[0:rows, :] = packed_ref[...]
    river_rows(xsend_ref, rows, 2 * pad, cells.astype(F32))
    river_rows(xsend_ref, rows, 2 * pad + wide, reaches.astype(F32))
    river_rows(xsend_ref, rows, 2 * pad + 2 * wide, outflow_ref[0])
    y_hot = hot(cells >> log2(cols), rows).astype(F32)
    y_hot3 = jnp.concatenate([y_hot, y_hot, y_hot], 0).astype(BF16)
    parts = jnp.concatenate(split3(inc_ref[0]), 0).astype(BF16)
    picked = lax.dot_general(parts, y_hot3, (((0,), (0,)), ((), ())), preferred_element_type=F32)
    values = jnp.sum(jnp.where(hot(cells & (cols - 1), cols), picked, 0.0), 0, keepdims=True)
    terms = stack3(inflow_ref[0] * values, 16)
    x_index = lax.axis_index("tx")
    owner = lax.broadcasted_iota(jnp.int32, (1, LANES), 1)
    stored = jnp.concatenate([storage_ref[0, :, 0:reach_local]] * (LANES // reach_local), 1)
    for c in range(reach_local * lax.axis_size("tx") // LANES):
        r_hot = hot(reaches, LANES, c * LANES).astype(F32).astype(BF16)
        total = lax.dot_general(terms, r_hot, (((1,), (1,)), ((), ())), preferred_element_type=F32)
        xsend_ref[pl.ds(rows + c, 1), :] = jnp.sum(total, 0, keepdims=True)
        xsend_ref[pl.ds(rows + pad + c, 1), :] = jnp.where(
            (owner + c * LANES) // reach_local == x_index, stored, 0.0
        )


def prefix_step(k, received, prior):
    upper = bit_of("ty", k) == 1
    if prior is None:
        return jnp.where(upper, received[0], 1.0), jnp.where(upper, received[1], 0.0)
    product = jnp.where(upper, prior[0] * received[0], prior[0])
    value = jnp.where(upper, prior[0] * received[1] + prior[1], prior[1])
    return product, value


def between_kernel(k, layers, sent_ref, got_ref, *refs):
    prior_ref = refs[0] if k > 0 else None
    send_ref, next_ref = refs[-2:]
    upper = bit_of("ty", k) == 1
    product, value = prefix_step(k, got_ref, prior_ref)
    next_ref[0] = product
    next_ref[1] = value
    own_a, own_b, got_a, got_b = sent_ref[0], sent_ref[1], got_ref[0], got_ref[1]
    low_b = jnp.where(upper, got_b, own_b)
    up_a = jnp.where(upper, own_a, got_a)
    up_b = jnp.where(upper, own_b, got_b)
    send_ref[0] = own_a * got_a
    send_ref[1] = up_a * low_b + up_b
    for layer in range(layers):
        passed = got_ref[2 + layer]
        if k == 0:
            passed = jnp.where(upper, passed, got_ref[2 + layers + layer])
        send_ref[2 + layer] = passed


def beside_x(received, rows):
    index = lax.axis_index("tx")
    below = jnp.zeros((rows, LANES), F32)
    above = below
    for k, buffer in enumerate(received):
        low = (1 << k) - 1
        full = (2 << k) - 1
        above = jnp.where((index & full) == low, buffer[0:rows, :], above)
        below = jnp.where((index & full) == low + 1, buffer[0:rows, :], below)
    return below, above


def multiply(u, blocks, inc_refs, total):
    for j in range(len(inc_refs)):
        total = total + blocks[j].astype(F32) * inc_refs[j][...]
    return total


def ahead_kernel(unknowns, count, blocks_hbm, *refs):
    inc_refs = refs[1:1 + unknowns]
    out_refs = refs[1 + unknowns:-2]
    blocks_ref, sems = refs[-2:]
    copies = fetch([(blocks_hbm.at[i], blocks_ref.at[i]) for i in range(count)], sems)
    for u in range(count):
        if u % WAITS == 0:
            for copy in copies[u:u + WAITS]:
                copy.wait()
        out_refs[u][...] = multiply(u, blocks_ref.at[u], inc_refs, jnp.zeros(out_refs[u].shape, F32))


def local_kernel(x_rounds, pad, reach_rows, slots, unknowns, layers, count, blocks_hbm, inc_hbm, dec_hbm, sent_ref, *refs):
    received, refs = refs[:x_rounds], refs[x_rounds:]
    inc_refs, refs = refs[:unknowns], refs[unknowns:]
    face_refs, refs = refs[:3 * layers], refs[3 * layers:]
    done_refs, refs = refs[:count], refs[count:]
    out_refs, refs = refs[:unknowns], refs[unknowns:]
    grown_refs, refs = refs[:unknowns], refs[unknowns:]
    blocks_ref, flux_ref, top_ref, dec_ref, value_ref, product_ref, sems = refs
    _, rows, cols = inc_refs[0].shape
    copies = fetch(
        [(inc_hbm.at[:, 0], top_ref), (dec_hbm, dec_ref)]
        + [(blocks_hbm.at[i], blocks_ref.at[i - count]) for i in range(count, unknowns)],
        sems,
    )
    lane = lax.broadcasted_iota(jnp.int32, (rows, cols), 1)
    wide = slots // LANES

    def slot_row(at):
        start = rows + 2 * pad + at * wide
        return jnp.concatenate([sent_ref[start + c:start + c + 1, :] for c in range(wide)], 1)

    cells = slot_row(0).astype(jnp.int32)
    reaches = slot_row(1).astype(jnp.int32)
    totals = sent_ref[rows:rows + pad, :] + received[-1][rows:rows + pad, :]
    storage = sent_ref[rows + pad:rows + 2 * pad, :] + received[-1][rows + pad:rows + 2 * pad, :]
    shift = log2(cols)
    picked = jnp.zeros((16, slots), F32)
    for c in range(reach_rows):
        section = stack3(totals[c:c + 1] / storage[c:c + 1], 16)
        r_hot = hot(reaches, LANES, c * LANES).astype(F32).astype(BF16)
        picked = picked + lax.dot_general(section, r_hot, (((1,), (0,)), ((), ())), preferred_element_type=F32)
    back = slot_row(2) * jnp.sum(picked, 0, keepdims=True)
    y_hot = hot(cells >> shift, rows)
    spread = jnp.concatenate([jnp.where(y_hot, part, 0.0) for part in split3(back)], 0).astype(BF16)
    x_hot = hot(cells & (cols - 1), cols).astype(F32).astype(BF16)
    added = lax.dot_general(spread, x_hot, (((1,), (1,)), ((), ())), preferred_element_type=F32)
    river = added[0:rows] + added[rows:2 * rows] + added[2 * rows:3 * rows]
    left, right = beside_x(received, rows)
    rim = jnp.where(lane & 1 == 0, pltpu.roll(right, cols - 1, 1), pltpu.roll(left, 1, 1))
    planes = unknowns * layers
    for layer in range(layers):
        face_x = face_refs[layer][...]
        face_y = face_refs[layers + layer][...]
        face_z = face_refs[2 * layers + layer][...]
        face_left = pltpu.roll(rim, (cols - 1 - 2 * (planes + layer)) % cols, 1)
        for first in range(0, unknowns, GROUP):
            group = range(first, min(first + GROUP, unknowns))
            here = jnp.stack([inc_refs[u][layer] for u in group])
            beside = jnp.stack([pltpu.roll(rim, cols - 1 - 2 * (u * layers + layer), 1) for u in group])
            flow_x = face_x * (here - jnp.where(lane == cols - 1, beside, pltpu.roll(here, cols - 1, 2)))
            from_left = jnp.where(lane == 0, face_left * (beside - here), pltpu.roll(flow_x, 1, 2))
            flow_y = face_y * (here - pltpu.roll(here, rows - 1, 1))
            total = flow_x - from_left + (flow_y - pltpu.roll(flow_y, 1, 1))
            if layer + 1 < layers:
                total = total + face_z * (here - jnp.stack([inc_refs[u][layer + 1] for u in group]))
            else:
                total = total + face_z * here
            if layer > 0:
                over = jnp.stack([inc_refs[u][layer - 1] for u in group])
                total = total + face_refs[2 * layers + layer - 1][...] * (here - over)
            for u in group:
                flux_ref[u, layer] = total[u - first] + river if u + layer == 0 else total[u - first]
    copies[0].wait()
    copies[1].wait()
    product = 0.1 * dec_ref[:, 0, :]
    value = 0.1 * top_ref[:, 0, :]
    product_ref[:, 0, :] = product
    value_ref[:, 0, :] = value
    for y in range(1, rows):
        decay = dec_ref[:, y, :]
        product = product * decay
        value = value * decay + 0.1 * top_ref[:, y, :]
        product_ref[:, y, :] = product
        value_ref[:, y, :] = value
    for u in range(unknowns):
        total = flux_ref[u]
        if u < count:
            total = total + done_refs[u][...]
        else:
            at = u - count
            if at % WAITS == 0:
                for copy in copies[2 + at:2 + at + WAITS]:
                    copy.wait()
            total = multiply(u, blocks_ref.at[at], inc_refs, total)
        out_refs[u][0] = total[0] + value_ref[u]
        out_refs[u][1:] = total[1:]
        grown_refs[u][...] = product_ref[u]


def final_kernel(unknowns, y_rounds, *refs):
    part_refs = refs[:unknowns]
    grown_refs = refs[unknowns:2 * unknowns]
    own_ref = refs[2 * unknowns]
    got = refs[2 * unknowns + 1:2 * unknowns + 1 + y_rounds]
    prior_ref, out_ref = refs[-2:]
    layers, rows, cols = part_refs[0].shape
    _, carry = prefix_step(y_rounds - 1, got[-1], prior_ref)
    index = lax.axis_index("ty")
    odd = (index & 1) == 1
    at = lax.broadcasted_iota(jnp.int32, (8, cols), 0)
    starts = []
    ends = []
    for layer in range(layers):
        passed_up = jnp.zeros(carry.shape, F32)
        passed_down = passed_up
        for k in range(1, y_rounds):
            full = (2 << k) - 1
            passed_up = jnp.where((index & full) == (1 << k), got[k][2 + layer], passed_up)
            passed_down = jnp.where((index & full) == (1 << k) - 1, got[k][2 + layer], passed_down)
        below = jnp.where(odd, got[0][2 + layers + layer], passed_up)
        above = jnp.where(odd, passed_down, got[0][2 + layer])
        low_face = below[unknowns:unknowns + 1]
        top_face = own_ref[2 + layers + layer, unknowns:unknowns + 1]
        starts.append(low_face * (own_ref[2 + layer] - below))
        ends.append(top_face * (own_ref[2 + layers + layer] - above))
    for u in range(unknowns):
        for layer in range(layers):
            total = part_refs[u][layer]
            if layer == 0:
                total = total + grown_refs[u][...] * carry[u:u + 1]
            head = total[0:8] + jnp.where(at == 0, starts[layer][u:u + 1], 0.0)
            foot = total[rows - 8:rows] + jnp.where(at == 7, ends[layer][u:u + 1], 0.0)
            out_ref[u, layer, 0:8, :] = head
            out_ref[u, layer, 8:rows - 8, :] = total[8:rows - 8]
            out_ref[u, layer, rows - 8:rows, :] = foot


def call(kernel, outs, args, far=0, scratch=(), grant=32 * 1024, cost=0):
    vmem = pl.BlockSpec(memory_space=pltpu.VMEM)
    hbm = pl.BlockSpec(memory_space=pltpu.HBM)
    return pl.pallas_call(
        kernel,
        out_shape=[jax.ShapeDtypeStruct(o.shape, o.dtype) for o in outs],
        in_specs=[hbm] * far + [vmem] * (len(args) - far),
        out_specs=[vmem] * len(outs),
        scratch_shapes=list(scratch),
        compiler_params=pltpu.CompilerParams(vmem_limit_bytes=grant * 1024),
        cost_estimate=pl.CostEstimate(flops=0, bytes_accessed=cost, transcendentals=0),
    )(*args)


def f32(*shape):
    return jax.ShapeDtypeStruct(shape, F32)


def like(a, *shape):
    return pltpu.VMEM(shape or a.shape, a.dtype)


SUMMARY_GRANT = 54600
LOCAL_GRANT = 53725
LOCAL_COST = 0
RIVER_COST = 0
GROUP = 7
WAITS = 3
AHEAD = 6
AHEAD_GRANT = 52000


def body(
    increment,
    blocks,
    face_weights,
    connected,
    overland_decay,
    river_cell,
    river_reach,
    river_count,
    inflow,
    outflow,
    storage,
):
    unknowns, layers, rows, cols = increment.shape
    x_size = lax.axis_size("tx")
    y_size = lax.axis_size("ty")
    x_rounds = log2(x_size)
    y_rounds = log2(y_size)
    slots = river_cell.shape[2]
    decay = jnp.swapaxes(overland_decay, 1, 2)
    reach_rows = storage.shape[1] * x_size // LANES
    pad = -(-reach_rows // 8) * 8
    tall = -(-(unknowns + 1) // 8) * 8
    plane = f32(rows, cols)
    y_first, packed, *kept = call(
        functools.partial(summary_kernel, unknowns),
        [f32(2 + 2 * layers, tall, cols), plane] + [f32(layers, rows, cols)] * unknowns + [plane] * (3 * layers),
        [increment, decay, face_weights, connected],
        far=4,
        scratch=[
            like(increment), like(decay), like(face_weights), like(connected), pltpu.SemaphoreType.DMA((4,)),
        ],
        grant=SUMMARY_GRANT,
    )
    live = lax.broadcasted_iota(jnp.int32, river_cell.shape, 2) < river_count[:, :, None]
    code = jnp.where(live, (river_cell + (rows * cols) * river_reach).astype(F32), 0.0)
    reach_local = storage.shape[1]
    stored = jnp.pad(storage[None], ((0, 0), (0, 0), (0, slots - reach_local)))
    stored = jnp.where(lax.broadcasted_iota(jnp.int32, stored.shape, 2) < reach_local, stored, jnp.where(live, 1.0, 0.0))
    (x_send,) = call(
        functools.partial(river_kernel, pad, reach_local),
        [f32(rows + 2 * pad + -(-3 * slots // LANES // 8) * 8, cols)],
        [code, jnp.where(live, outflow, 0.0), jnp.where(live, inflow, 0.0), stored, packed, kept[0], y_first],
        cost=RIVER_COST,
    )
    y_send = y_first
    y_got = []
    x_got = []
    prior = None
    at = lax.broadcasted_iota(jnp.int32, x_send.shape, 0)
    summed = (at >= rows) & (at < rows + 2 * pad)
    for k in range(max(x_rounds, y_rounds)):
        if k < y_rounds:
            y_got.append(lax.ppermute(y_send, "ty", [(i, i ^ (1 << k)) for i in range(y_size)]))
        if k < x_rounds:
            x_got.append(lax.ppermute(x_send, "tx", [(i, i ^ ((2 << k) - 1)) for i in range(x_size)]))
            if k + 1 < x_rounds:
                x_send = x_send + jnp.where(summed, x_got[-1], 0.0)
        if k + 1 < y_rounds:
            y_send, prior = call(
                functools.partial(between_kernel, k, layers),
                [f32(2 + layers, tall, cols), f32(2, tall, cols)],
                [y_send, y_got[-1]] + ([prior] + x_got[k:k + 1] + list(ahead[:1]) if k > 0 else []),
            )
            if k == 0:
                ahead = call(
                    functools.partial(ahead_kernel, unknowns, AHEAD),
                    [f32(layers, rows, cols)] * AHEAD,
                    [blocks, y_send, *kept[:unknowns]],
                    far=1,
                    scratch=[like(blocks, AHEAD, *blocks.shape[1:]), pltpu.SemaphoreType.DMA((AHEAD,))],
                    grant=AHEAD_GRANT,
                )
    local = call(
        functools.partial(local_kernel, x_rounds, pad, reach_rows, slots, unknowns, layers, AHEAD),
        [f32(layers, rows, cols)] * unknowns + [plane] * unknowns,
        [blocks, increment, decay, x_send, *x_got, *kept, *ahead],
        far=3,
        scratch=[
            like(blocks, unknowns - AHEAD, *blocks.shape[1:]), like(increment), like(decay), like(decay), like(decay), like(decay), pltpu.SemaphoreType.DMA((2 + unknowns - AHEAD,)),
        ],
        grant=LOCAL_GRANT,
        cost=LOCAL_COST,
    )
    (total,) = call(
        functools.partial(final_kernel, unknowns, y_rounds),
        [increment],
        [*local, y_first, *y_got, prior],
    )
    return total


def solution(mesh):
    in_specs = (
        P(None, None, "ty", "tx"),
        P(None, None, None, "ty", "tx"),
        P(None, None, "ty", "tx"),
        P(None, None, "ty", "tx"),
        P(None, "tx", "ty"),
        P("tx", "ty", None),
        P("tx", "ty", None),
        P("tx", "ty"),
        P("tx", "ty", None),
        P("tx", "ty", None),
        P("ty", "tx"),
    )
    out_specs = P(None, None, "ty", "tx")
    return jax.shard_map(body, mesh=mesh, in_specs=in_specs, out_specs=out_specs, check_vma=False)
```

time: 22.4 us -> 18.7 us (0.83)
  waiting for transfers between devices: 3.93 us -> 0.57 us
  other arithmetic: 0 us -> 1.5 us
  Pallas kernels: 8.43 us -> 6.95 us
  local copies, waits for them, and re-layouts: 0.75 us -> 0 us
  starting transfers between devices: 8.38 us -> 8.69 us
    ppermute x2, waiting for transfers between devices: 3.92 us -> 0.56 us  [body(): lax.ppermute(x_send, 'tx', [(i, i ^ (2 << k) - 1) for i in range(x_size)])]
    pallas_call x6 -> x7, Pallas kernels: 8.43 us -> 6.95 us  [call(): pl.pallas_call(kernel, out_shape=[jax.ShapeDtypeStruct(o.shape, o.dtype)...]
    select_n x0 -> x2, other arithmetic: none -> 1.42 us  [the longest x1 0.72 us: body(): jnp.where(lax.broadcasted_iota(jnp.int32, stored.shape, 2) < reach_local,...]
    unnamed x2 -> x0, local copies, waits for them, and re-layouts: 0.75 us -> none
  transfers between devices with their start and end apart: 5 -> 5, of which waited for: 2 -> 1; matrix products, arithmetic and copies ran while one was open for 0% -> 8% of each run, Pallas kernels for 28% -> 24%
where the time goes in v1:
time: 18.7 us; the launch traced here: 18.4 us
  starting transfers between devices  8.69 us (46%)
  Pallas kernels  6.95 us (37%)
  other arithmetic  1.5 us (8%)
  between operations  0.72 us (4%)
  waiting for transfers between devices  0.57 us (3%)
    ppermute x3, starting transfers between devices, body(): lax.ppermute(y_send, 'ty', [(i, i ^ 1 << k) for i in range(y_size)])  7.44 us
    pallas_call x7, Pallas kernels, call(): pl.pallas_call(kernel, out_shape=[jax.ShapeDtypeStruct(o.shape, o.dtype)...  6.95 us
    ppermute x2, starting transfers between devices, body(): lax.ppermute(x_send, 'tx', [(i, i ^ (2 << k) - 1) for i in range(x_size)])  1.25 us
    select_n x1, other arithmetic, body(): jnp.where(lax.broadcasted_iota(jnp.int32, stored.shape, 2) < reach_local,...  0.72 us
    select_n x1, other arithmetic, body(): jnp.where(live, inflow, 0.0)  0.7 us
    ppermute x2, waiting for transfers between devices, body(): lax.ppermute(x_send, 'tx', [(i, i ^ (2 << k) - 1) for i in range(x_size)])  0.56 us
  transfers between devices with their start and end apart: 5, of which 1 were waited for; matrix products, arithmetic and copies ran while one was open for 8% of the time, Pallas kernels for 24%

profile of v1, /device:TPU:0, one launch (start us, length us, event | category | flops | bytes accessed | tf_op | source)
XLA Modules:
  0.0 18.4 jit_solution(13974453987698446509)
XLA Ops:
  0.0 1.6 %shard_map.109 = (f32[6,16,128]{2,1,0:T(8,128)S(1)}, f32[32,128]{1,0:T(8,128)S(1)}, f32[2,32,128]{2,1,0:T(8,128)S(1)}, f32[2,32,128]{2,1,0:T(8,128)S(1)}, f32[2,...) custom-call(f32[13,2,32,128]{3,2,1,0:T(8,128)} %inc_hbm.3, ...), custom_call_target="tpu_custom_call" | custom-call | tf_op jit(solution)/shard_map/pallas_call | solution.py:312
  1.6 3.0 %collective-permute-start.2 = (f32[6,16,128]{2,1,0:T(8,128)S(1)}, f32[6,16,128]{2,1,0:T(8,128)S(1)}, u32[]{:S(2)}, u32[]{:S(2)}) collective-permute-start(f32[6,16,128]{2,1,0:T(8,128)S(1)} %get-tuple-element.64._.sent_ref.refs_26_), channel_id=1, source_target_pairs={{0,1},{1,0},{2,3},{3,2},{4,5},{5,4},{6,7},{7,6},{8,9},{9,8},{10,11... | collective-permute-start | bytes 147464 | tf_op jit(solution)/shard_map/ppermute | solution.py:394
  5.2 0.7 %fusion = (f32[1,1,256]{2,1,0:T(1,128)S(1)}, f32[1,1,256]{2,1,0:T(1,128)S(1)}) fusion(f32[1,1,256]{2,1,0:T(1,128)} %param.19, s32[]{:T(128)} %bitcast.4, f32[1,1,256]{2,1,0:T(1,128)} %param.20), kind=kLoop, calls=%fused_computation.5 | loop fusion | flops 768 | bytes 4100 | tf_op jit(solution)/shard_map/jit(_where)/select_n | solution.py:383
  5.9 0.7 %compare_select_fusion = (f32[1,1,256]{2,1,0:T(1,128)S(1)}, f32[1,1,256]{2,1,0:T(1,128)S(1)}) fusion(f32[1,1,64]{2,1,0:T(1,128)} %bitcast.7, s32[]{:T(128)} %bitcast.3, s32[1,1,256]{2,1,0:T(1,128)} %param.16, s32[1,1,256]{2,1,0:T(1,128)} %param.17), kind=kLoop, calls=%fused_computation.1 | loop fusion | flops 2048 | bytes 4356 | tf_op jit(solution)/shard_map/jit(_where)/select_n | solution.py:379
  6.7 0.3 %shard_map.110 = f32[56,128]{1,0:T(8,128)S(1)} custom-call(f32[1,1,256]{2,1,0:T(1,128)S(1)} %get-tuple-element.120.code_ref, f32[1,1,256]{2,1,0:T(1,128)S(1)} %get-tuple-element.122.outflow_ref, f32[1,1,256]{2,1,0:T(1,128)S(1)} %get-tuple-element.121.inflow_ref, f32[1,1,256]{2,1,0:T(1,128)S(1)} %get-tuple-element.119.storage_ref, ...), custom_call_target="tpu_custom_call" | custom-call | tf_op jit(solution)/shard_map/pallas_call | solution.py:312
  7.0 0.0 collective-permute-start
  7.0 0.0 collective-permute-done.2.got_ref.refs_27_
  7.1 1.8 %collective-permute-start.3 = (f32[4,16,128]{2,1,0:T(8,128)S(1)}, f32[4,16,128]{2,1,0:T(8,128)S(1)}, u32[]{:S(2)}, u32[]{:S(2)}) collective-permute-start(f32[4,16,128]{2,1,0:T(8,128)S(1)} %get-tuple-element.83.refs_0_.sent_ref), channel_id=1, source_target_pairs={{0,2},{1,3},{2,0},{3,1},{4,6},{5,7},{6,4},{7,5},{8,10},{9,11},{10,... | collective-permute-start | bytes 98312 | tf_op jit(solution)/shard_map/ppermute | solution.py:394
  8.8 0.0 collective-permute-done.refs_0_
  8.8 0.1 select_add_fusion.sent_ref
  8.9 1.2 %collective-permute-start.1 = (f32[56,128]{1,0:T(8,128)S(1)}, f32[56,128]{1,0:T(8,128)S(1)}, u32[]{:S(2)}, u32[]{:S(2)}) collective-permute-start(f32[56,128]{1,0:T(8,128)S(1)} %select_add_fusion.sent_ref), channel_id=1, source_target_pairs={{0,24},{8,16},{16,8},{24,0},{1,25},{9,17},{17,9},{25,1},{2,26},{10... | collective-permute-start | bytes 86024 | tf_op jit(solution)/shard_map/ppermute | solution.py:396
  10.2 1.6 %shard_map.112 = (f32[2,32,128]{2,1,0:T(8,128)S(1)}, f32[2,32,128]{2,1,0:T(8,128)S(1)}, f32[2,32,128]{2,1,0:T(8,128)S(1)}, f32[2,32,128]{2,1,0:T(8,128)S(1)}, f3...) custom-call(bf16[13,13,2,32,128]{4,3,2,1,0:T(8,128)(2,1)} %blocks_hbm.3, ...), custom_call_target="tpu_custom_call" | custom-call | tf_op jit(solution)/shard_map/pallas_call | solution.py:312
  11.8 0.6 %collective-permute-done.1.refs_1_ = f32[56,128]{1,0:T(8,128)S(1)} collective-permute-done((f32[56,128]{1,0:T(8,128)S(1)}, f32[56,128]{1,0:T(8,128)S(1)}, u32[]{:S(2)}, u32[]{:S(2)}) %collective-permute-start.1) | collective-permute-done | bytes 28704 | tf_op jit(solution)/shard_map/ppermute | solution.py:396
  12.3 0.0 collective-permute-done.3.got_ref.refs_28_
  12.3 2.7 %collective-permute-start.4 = (f32[4,16,128]{2,1,0:T(8,128)S(1)}, f32[4,16,128]{2,1,0:T(8,128)S(1)}, u32[]{:S(2)}, u32[]{:S(2)}) collective-permute-start(f32[4,16,128]{2,1,0:T(8,128)S(1)} %get-tuple-element.117), channel_id=1, source_target_pairs={{0,4},{1,5},{2,6},{3,7},{4,0},{5,1},{6,2},{7,3},{8,12},{9,13},{10,... | collective-permute-start | bytes 98312 | tf_op jit(solution)/shard_map/ppermute | solution.py:394
  15.0 2.6 %shard_map.113 = (f32[2,32,128]{2,1,0:T(8,128)S(1)}, f32[2,32,128]{2,1,0:T(8,128)S(1)}, f32[2,32,128]{2,1,0:T(8,128)S(1)}, f32[2,32,128]{2,1,0:T(8,128)S(1)}, f3...) custom-call(bf16[13,13,2,32,128]{4,3,2,1,0:T(8,128)(2,1)} %blocks_hb, ...), custom_call_target="tpu_custom_call" | custom-call | tf_op jit(solution)/shard_map/pallas_call | solution.py:312
  17.6 0.0 collective-permute-done.4.refs_29_
  17.6 0.9 %shard_map.115 = f32[13,2,32,128]{3,2,1,0:T(8,128)} custom-call(f32[2,32,128]{2,1,0:T(8,128)S(1)} %get-tuple-element.90.refs_0_, f32[2,32,128]{2,1,0:T(8,128)S(1)} %get-tuple-element.91.refs_1_, f32[2,32,128]{2,1,0:T(8,128)S(1)} %get-tuple-element.92.refs_2_, f32[2,32,128]{2,1,0:T(8,128)S(1)} %get-tuple-element.93.refs_3_, ...), custom_call_target="tpu_custom_call" | custom-call | tf_op jit(solution)/shard_map/pallas_call | solution.py:312
  (3 shorter events, 0.0 us)
Async XLA Ops:
  1.6 5.4 %collective-permute-start.2 = (f32[6,16,128]{2,1,0:T(8,128)S(1)}, f32[6,16,128]{2,1,0:T(8,128)S(1)}, u32[]{:S(2)}, u32[]{:S(2)}) collective-permute-start(f32[6,16,128]{2,1,0:T(8,128)S(1)} %get-tuple-element.64._.sent_ref.refs_26_), channel_id=1, source_target_pairs={{0,1},{1,0},{2,3},{3,2},{4,5},{5,4},{6,7},{7,6},{8,9},{9,8},{10,11... | collective-permute-start | bytes 147464 | tf_op jit(solution)/shard_map/ppermute | solution.py:394
  7.0 1.8 %collective-permute-start = (f32[56,128]{1,0:T(8,128)S(1)}, f32[56,128]{1,0:T(8,128)S(1)}, u32[]{:S(2)}, u32[]{:S(2)}) collective-permute-start(f32[56,128]{1,0:T(8,128)S(1)} %shard_map.110), channel_id=1, source_target_pairs={{0,8},{8,0},{16,24},{24,16},{1,9},{9,1},{17,25},{25,17},{2,10},{10... | collective-permute-start | bytes 86024 | tf_op jit(solution)/shard_map/ppermute | solution.py:396
  7.1 5.3 %collective-permute-start.3 = (f32[4,16,128]{2,1,0:T(8,128)S(1)}, f32[4,16,128]{2,1,0:T(8,128)S(1)}, u32[]{:S(2)}, u32[]{:S(2)}) collective-permute-start(f32[4,16,128]{2,1,0:T(8,128)S(1)} %get-tuple-element.83.refs_0_.sent_ref), channel_id=1, source_target_pairs={{0,2},{1,3},{2,0},{3,1},{4,6},{5,7},{6,4},{7,5},{8,10},{9,11},{10,... | collective-permute-start | bytes 98312 | tf_op jit(solution)/shard_map/ppermute | solution.py:394
  8.9 3.4 %collective-permute-start.1 = (f32[56,128]{1,0:T(8,128)S(1)}, f32[56,128]{1,0:T(8,128)S(1)}, u32[]{:S(2)}, u32[]{:S(2)}) collective-permute-start(f32[56,128]{1,0:T(8,128)S(1)} %select_add_fusion.sent_ref), channel_id=1, source_target_pairs={{0,24},{8,16},{16,8},{24,0},{1,25},{9,17},{17,9},{25,1},{2,26},{10... | collective-permute-start | bytes 86024 | tf_op jit(solution)/shard_map/ppermute | solution.py:396
  12.3 5.2 %collective-permute-start.4 = (f32[4,16,128]{2,1,0:T(8,128)S(1)}, f32[4,16,128]{2,1,0:T(8,128)S(1)}, u32[]{:S(2)}, u32[]{:S(2)}) collective-permute-start(f32[4,16,128]{2,1,0:T(8,128)S(1)} %get-tuple-element.117), channel_id=1, source_target_pairs={{0,4},{1,5},{2,6},{3,7},{4,0},{5,1},{6,2},{7,3},{8,12},{9,13},{10,... | collective-permute-start | bytes 98312 | tf_op jit(solution)/shard_map/ppermute | solution.py:394

commit v2 on v1

--- a/solution.py
+++ b/solution.py
@@ -140,13 +140,15 @@
     low_b = jnp.where(upper, got_b, own_b)
     up_a = jnp.where(upper, own_a, got_a)
     up_b = jnp.where(upper, own_b, got_b)
-    send_ref[0] = own_a * got_a
-    send_ref[1] = up_a * low_b + up_b
+    lead = send_ref.shape[0] - layers
+    send_ref[lead - 1] = up_a * low_b + up_b
+    if lead == 2:
+        send_ref[0] = own_a * got_a
     for layer in range(layers):
         passed = got_ref[2 + layer]
         if k == 0:
             passed = jnp.where(upper, passed, got_ref[2 + layers + layer])
-        send_ref[2 + layer] = passed
+        send_ref[lead + layer] = passed
 
 
 def beside_x(received, rows):
@@ -167,30 +169,51 @@
     return total
 
 
-def ahead_kernel(unknowns, count, blocks_hbm, *refs):
-    inc_refs = refs[1:1 + unknowns]
-    out_refs = refs[1 + unknowns:-2]
-    blocks_ref, sems = refs[-2:]
-    copies = fetch([(blocks_hbm.at[i], blocks_ref.at[i]) for i in range(count)], sems)
-    for u in range(count):
+def ahead_kernel(unknowns, count, blocks_hbm, dec_hbm, *refs):
+    inc_refs, refs = refs[2:2 + unknowns], refs[2 + unknowns:]
+    out_refs, refs = refs[:unknowns], refs[unknowns:]
+    grown_refs, refs = refs[:unknowns], refs[unknowns:]
+    blocks_ref, top_ref, dec_ref, value_ref, product_ref, sems = refs
+    _, rows, cols = top_ref.shape
+    copies = fetch(
+        [(dec_hbm, dec_ref)] + [(blocks_hbm.at[i], blocks_ref.at[i]) for i in range(count)], sems
+    )
+    for u in range(unknowns):
+        top_ref[u] = inc_refs[u][0]
+    copies[0].wait()
+    product = 0.1 * dec_ref[:, 0, :]
+    value = 0.1 * top_ref[:, 0, :]
+    product_ref[:, 0, :] = product
+    value_ref[:, 0, :] = value
+    for y in range(1, rows):
+        decay = dec_ref[:, y, :]
+        product = product * decay
+        value = value * decay + 0.1 * top_ref[:, y, :]
+        product_ref[:, y, :] = product
+        value_ref[:, y, :] = value
+    for u in range(unknowns):
+        grown_refs[u][...] = product_ref[u]
+        if u >= count:
+            out_refs[u][...] = value_ref[u]
+            continue
         if u % WAITS == 0:
-            for copy in copies[u:u + WAITS]:
+            for copy in copies[1 + u:1 + min(u + WAITS, count)]:
                 copy.wait()
-        out_refs[u][...] = multiply(u, blocks_ref.at[u], inc_refs, jnp.zeros(out_refs[u].shape, F32))
-
-
-def local_kernel(x_rounds, pad, reach_rows, slots, unknowns, layers, count, blocks_hbm, inc_hbm, dec_hbm, sent_ref, *refs):
+        total = multiply(u, blocks_ref.at[u], inc_refs, jnp.zeros(out_refs[u].shape, F32))
+        out_refs[u][0] = total[0] + value_ref[u]
+        out_refs[u][1:] = total[1:]
+
+
+def local_kernel(x_rounds, pad, reach_rows, slots, unknowns, layers, count, blocks_hbm, sent_ref, *refs):
     received, refs = refs[:x_rounds], refs[x_rounds:]
     inc_refs, refs = refs[:unknowns], refs[unknowns:]
     face_refs, refs = refs[:3 * layers], refs[3 * layers:]
-    done_refs, refs = refs[:count], refs[count:]
+    done_refs, refs = refs[:unknowns], refs[unknowns:]
     out_refs, refs = refs[:unknowns], refs[unknowns:]
-    grown_refs, refs = refs[:unknowns], refs[unknowns:]
-    blocks_ref, flux_ref, top_ref, dec_ref, value_ref, product_ref, sems = refs
+    blocks_ref, flux_ref, sems = refs
     _, rows, cols = inc_refs[0].shape
     copies = fetch(
-        [(inc_hbm.at[:, 0], top_ref), (dec_hbm, dec_ref)]
-        + [(blocks_hbm.at[i], blocks_ref.at[i - count]) for i in range(count, unknowns)],
+        [(blocks_hbm.at[i], blocks_ref.at[i - count]) for i in range(count, unknowns)],
         sems,
     )
     lane = lax.broadcasted_iota(jnp.int32, (rows, cols), 1)
@@ -241,31 +264,18 @@
                 total = total + face_refs[2 * layers + layer - 1][...] * (here - over)
             for u in group:
                 flux_ref[u, layer] = total[u - first] + river if u + layer == 0 else total[u - first]
-    copies[0].wait()
-    copies[1].wait()
-    product = 0.1 * dec_ref[:, 0, :]
-    value = 0.1 * top_ref[:, 0, :]
-    product_ref[:, 0, :] = product
-    value_ref[:, 0, :] = value
-    for y in range(1, rows):
-        decay = dec_ref[:, y, :]
-        product = product * decay
-        value = value * decay + 0.1 * top_ref[:, y, :]
-        product_ref[:, y, :] = product
-        value_ref[:, y, :] = value
     for u in range(unknowns):
         total = flux_ref[u]
         if u < count:
-            total = total + done_refs[u][...]
-        else:
-            at = u - count
-            if at % WAITS == 0:
-                for copy in copies[2 + at:2 + at + WAITS]:
-                    copy.wait()
-            total = multiply(u, blocks_ref.at[at], inc_refs, total)
-        out_refs[u][0] = total[0] + value_ref[u]
+            out_refs[u][...] = total + done_refs[u][...]
+            continue
+        at = u - count
+        if at % WAITS == 0:
+            for copy in copies[at:at + WAITS]:
+                copy.wait()
+        total = multiply(u, blocks_ref.at[at], inc_refs, total)
+        out_refs[u][0] = total[0] + done_refs[u][...]
         out_refs[u][1:] = total[1:]
-        grown_refs[u][...] = product_ref[u]
 
 
 def final_kernel(unknowns, y_rounds, *refs):
@@ -275,7 +285,8 @@
     got = refs[2 * unknowns + 1:2 * unknowns + 1 + y_rounds]
     prior_ref, out_ref = refs[-2:]
     layers, rows, cols = part_refs[0].shape
-    _, carry = prefix_step(y_rounds - 1, got[-1], prior_ref)
+    upper = bit_of("ty", y_rounds - 1) == 1
+    carry = jnp.where(upper, prior_ref[0] * got[-1][0] + prior_ref[1], prior_ref[1])
     index = lax.axis_index("ty")
     odd = (index & 1) == 1
     at = lax.broadcasted_iota(jnp.int32, (8, cols), 0)
@@ -286,8 +297,8 @@
         passed_down = passed_up
         for k in range(1, y_rounds):
             full = (2 << k) - 1
-            passed_up = jnp.where((index & full) == (1 << k), got[k][2 + layer], passed_up)
-            passed_down = jnp.where((index & full) == (1 << k) - 1, got[k][2 + layer], passed_down)
+            passed_up = jnp.where((index & full) == (1 << k), got[k][got[k].shape[0] - layers + layer], passed_up)
+            passed_down = jnp.where((index & full) == (1 << k) - 1, got[k][got[k].shape[0] - layers + layer], passed_down)
         below = jnp.where(odd, got[0][2 + layers + layer], passed_up)
         above = jnp.where(odd, passed_down, got[0][2 + layer])
         low_face = below[unknowns:unknowns + 1]
@@ -329,13 +340,14 @@
 
 
 SUMMARY_GRANT = 54600
-LOCAL_GRANT = 53725
+LOCAL_GRANT = 52000
 LOCAL_COST = 0
 RIVER_COST = 0
-GROUP = 7
-WAITS = 3
-AHEAD = 6
-AHEAD_GRANT = 52000
+GROUP = 13
+WAITS = 2
+AHEAD = 4
+EXTRA = 0
+AHEAD_GRANT = 54080
 
 
 def body(
@@ -379,7 +391,7 @@
     stored = jnp.where(lax.broadcasted_iota(jnp.int32, stored.shape, 2) < reach_local, stored, jnp.where(live, 1.0, 0.0))
     (x_send,) = call(
         functools.partial(river_kernel, pad, reach_local),
-        [f32(rows + 2 * pad + -(-3 * slots // LANES // 8) * 8, cols)],
+        [f32(EXTRA + rows + 2 * pad + -(-3 * slots // LANES // 8) * 8, cols)],
         [code, jnp.where(live, outflow, 0.0), jnp.where(live, inflow, 0.0), stored, packed, kept[0], y_first],
         cost=RIVER_COST,
     )
@@ -399,25 +411,30 @@
         if k + 1 < y_rounds:
             y_send, prior = call(
                 functools.partial(between_kernel, k, layers),
-                [f32(2 + layers, tall, cols), f32(2, tall, cols)],
-                [y_send, y_got[-1]] + ([prior] + x_got[k:k + 1] + list(ahead[:1]) if k > 0 else []),
+                [f32((2 if k + 2 < y_rounds else 1) + layers, tall, cols), f32(2, tall, cols)],
+                [y_send, y_got[-1]] + ([prior] + list(ahead[:1]) if k > 0 else []),
             )
             if k == 0:
-                ahead = call(
+                made = call(
                     functools.partial(ahead_kernel, unknowns, AHEAD),
-                    [f32(layers, rows, cols)] * AHEAD,
-                    [blocks, y_send, *kept[:unknowns]],
-                    far=1,
-                    scratch=[like(blocks, AHEAD, *blocks.shape[1:]), pltpu.SemaphoreType.DMA((AHEAD,))],
+                    [f32(layers, rows, cols)] * AHEAD + [plane] * (2 * unknowns - AHEAD),
+                    [blocks, decay, y_send, x_send, *kept[:unknowns]],
+                    far=2,
+                    scratch=[
+                        like(blocks, AHEAD, *blocks.shape[1:]), like(decay), like(decay), like(decay), like(decay),
+                        pltpu.SemaphoreType.DMA((1 + AHEAD,)),
+                    ],
                     grant=AHEAD_GRANT,
                 )
+                ahead, grown = made[:unknowns], made[unknowns:]
     local = call(
         functools.partial(local_kernel, x_rounds, pad, reach_rows, slots, unknowns, layers, AHEAD),
-        [f32(layers, rows, cols)] * unknowns + [plane] * unknowns,
-        [blocks, increment, decay, x_send, *x_got, *kept, *ahead],
-        far=3,
+        [f32(layers, rows, cols)] * unknowns,
+        [blocks, x_send, *x_got, *kept, *ahead],
+        far=1,
         scratch=[
-            like(blocks, unknowns - AHEAD, *blocks.shape[1:]), like(increment), like(decay), like(decay), like(decay), like(decay), pltpu.SemaphoreType.DMA((2 + unknowns - AHEAD,)),
+            like(blocks, unknowns - AHEAD, *blocks.shape[1:]), like(increment),
+            pltpu.SemaphoreType.DMA((unknowns - AHEAD,)),
         ],
         grant=LOCAL_GRANT,
         cost=LOCAL_COST,
@@ -425,7 +442,7 @@
     (total,) = call(
         functools.partial(final_kernel, unknowns, y_rounds),
         [increment],
-        [*local, y_first, *y_got, prior],
+        [*local, *grown, y_first, *y_got, prior],
     )
     return total
 

time: 18.7 us -> 17.9 us (0.957)
  waiting for transfers between devices: 0.57 us -> 0.01 us
  Pallas kernels: 6.95 us -> 6.75 us
    ppermute x2, waiting for transfers between devices: 0.56 us -> 0.01 us  [body(): lax.ppermute(x_send, 'tx', [(i, i ^ (2 << k) - 1) for i in range(x_size)])]
    pallas_call x7, Pallas kernels: 6.95 us -> 6.75 us  [call(): pl.pallas_call(kernel, out_shape=[jax.ShapeDtypeStruct(o.shape, o.dtype)...]
  transfers between devices with their start and end apart: 5 -> 5, of which waited for: 1 -> 0; matrix products, arithmetic and copies ran while one was open for 8% -> 8% of each run, Pallas kernels for 24% -> 24%
where the time goes in v2:
time: 17.9 us; the launch traced here: 17.7 us
  starting transfers between devices  8.69 us (49%)
  Pallas kernels  6.75 us (38%)
  other arithmetic  1.5 us (8%)
  between operations  0.73 us (4%)
    ppermute x3, starting transfers between devices, body(): lax.ppermute(y_send, 'ty', [(i, i ^ 1 << k) for i in range(y_size)])  7.44 us
    pallas_call x7, Pallas kernels, call(): pl.pallas_call(kernel, out_shape=[jax.ShapeDtypeStruct(o.shape, o.dtype)...  6.75 us
    ppermute x2, starting transfers between devices, body(): lax.ppermute(x_send, 'tx', [(i, i ^ (2 << k) - 1) for i in range(x_size)])  1.25 us
    select_n x1, other arithmetic, body(): jnp.where(lax.broadcasted_iota(jnp.int32, stored.shape, 2) < reach_local,...  0.72 us
    select_n x1, other arithmetic, body(): jnp.where(live, inflow, 0.0)  0.7 us
  transfers between devices with their start and end apart: 5, of which 0 were waited for; matrix products, arithmetic and copies ran while one was open for 8% of the time, Pallas kernels for 24%

profile of v2, /device:TPU:0, one launch (start us, length us, event | category | flops | bytes accessed | tf_op | source)
XLA Modules:
  0.0 17.7 jit_solution(1916372586530199779)
XLA Ops:
  0.0 1.6 %shard_map.109 = (f32[6,16,128]{2,1,0:T(8,128)S(1)}, f32[32,128]{1,0:T(8,128)S(1)}, f32[2,32,128]{2,1,0:T(8,128)S(1)}, f32[2,32,128]{2,1,0:T(8,128)S(1)}, f32[2,...) custom-call(f32[13,2,32,128]{3,2,1,0:T(8,128)} %inc_hbm.1, ...), custom_call_target="tpu_custom_call" | custom-call | tf_op jit(solution)/shard_map/pallas_call | solution.py:323
  1.6 3.0 %collective-permute-start.2 = (f32[6,16,128]{2,1,0:T(8,128)S(1)}, f32[6,16,128]{2,1,0:T(8,128)S(1)}, u32[]{:S(2)}, u32[]{:S(2)}) collective-permute-start(f32[6,16,128]{2,1,0:T(8,128)S(1)} %get-tuple-element.71._.sent_ref.refs_26_), channel_id=1, source_target_pairs={{0,1},{1,0},{2,3},{3,2},{4,5},{5,4},{6,7},{7,6},{8,9},{9,8},{10,11... | collective-permute-start | bytes 147464 | tf_op jit(solution)/shard_map/ppermute | solution.py:406
  5.2 0.7 %fusion = (f32[1,1,256]{2,1,0:T(1,128)S(1)}, f32[1,1,256]{2,1,0:T(1,128)S(1)}) fusion(f32[1,1,256]{2,1,0:T(1,128)} %param.19, s32[]{:T(128)} %bitcast.4, f32[1,1,256]{2,1,0:T(1,128)} %param.20), kind=kLoop, calls=%fused_computation.5 | loop fusion | flops 768 | bytes 4100 | tf_op jit(solution)/shard_map/jit(_where)/select_n | solution.py:395
  5.9 0.7 %compare_select_fusion = (f32[1,1,256]{2,1,0:T(1,128)S(1)}, f32[1,1,256]{2,1,0:T(1,128)S(1)}) fusion(f32[1,1,64]{2,1,0:T(1,128)} %bitcast.7, s32[]{:T(128)} %bitcast.3, s32[1,1,256]{2,1,0:T(1,128)} %param.16, s32[1,1,256]{2,1,0:T(1,128)} %param.17), kind=kLoop, calls=%fused_computation.1 | loop fusion | flops 2048 | bytes 4356 | tf_op jit(solution)/shard_map/jit(_where)/select_n | solution.py:391
  6.7 0.3 %shard_map.110 = f32[56,128]{1,0:T(8,128)S(1)} custom-call(f32[1,1,256]{2,1,0:T(1,128)S(1)} %get-tuple-element.134.code_ref, f32[1,1,256]{2,1,0:T(1,128)S(1)} %get-tuple-element.136.outflow_ref, f32[1,1,256]{2,1,0:T(1,128)S(1)} %get-tuple-element.135.inflow_ref, f32[1,1,256]{2,1,0:T(1,128)S(1)} %get-tuple-element.133.storage_ref, ...), custom_call_target="tpu_custom_call" | custom-call | tf_op jit(solution)/shard_map/pallas_call | solution.py:323
  7.0 0.0 collective-permute-start
  7.0 0.0 collective-permute-done.2.got_ref.refs_27_
  7.1 1.8 %collective-permute-start.3 = (f32[4,16,128]{2,1,0:T(8,128)S(1)}, f32[4,16,128]{2,1,0:T(8,128)S(1)}, u32[]{:S(2)}, u32[]{:S(2)}) collective-permute-start(f32[4,16,128]{2,1,0:T(8,128)S(1)} %get-tuple-element.90.refs_0_.sent_ref), channel_id=1, source_target_pairs={{0,2},{1,3},{2,0},{3,1},{4,6},{5,7},{6,4},{7,5},{8,10},{9,11},{10,... | collective-permute-start | bytes 98312 | tf_op jit(solution)/shard_map/ppermute | solution.py:406
  8.8 0.0 collective-permute-done.refs_0_
  8.8 0.1 select_add_fusion.refs_1_.sent_ref
  8.9 1.2 %collective-permute-start.1 = (f32[56,128]{1,0:T(8,128)S(1)}, f32[56,128]{1,0:T(8,128)S(1)}, u32[]{:S(2)}, u32[]{:S(2)}) collective-permute-start(f32[56,128]{1,0:T(8,128)S(1)} %select_add_fusion.refs_1_.sent_ref), channel_id=1, source_target_pairs={{0,24},{8,16},{16,8},{24,0},{1,25},{9,17},{17,9},{25,1},{2,26},{10... | collective-permute-start | bytes 86024 | tf_op jit(solution)/shard_map/ppermute | solution.py:408
  10.2 1.7 %shard_map.112 = (f32[2,32,128]{2,1,0:T(8,128)S(1)}, f32[2,32,128]{2,1,0:T(8,128)S(1)}, f32[2,32,128]{2,1,0:T(8,128)S(1)}, f32[2,32,128]{2,1,0:T(8,128)S(1)}, f3...) custom-call(bf16[13,13,2,32,128]{4,3,2,1,0:T(8,128)(2,1)} %blocks_hb, ...), custom_call_target="tpu_custom_call" | custom-call | tf_op jit(solution)/shard_map/pallas_call | solution.py:323
  11.8 0.0 collective-permute-done.3.got_ref.refs_28_
  11.9 2.7 %collective-permute-start.4 = (f32[3,16,128]{2,1,0:T(8,128)S(1)}, f32[3,16,128]{2,1,0:T(8,128)S(1)}, u32[]{:S(2)}, u32[]{:S(2)}) collective-permute-start(f32[3,16,128]{2,1,0:T(8,128)S(1)} %get-tuple-element.131), channel_id=1, source_target_pairs={{0,4},{1,5},{2,6},{3,7},{4,0},{5,1},{6,2},{7,3},{8,12},{9,13},{10,... | collective-permute-start | bytes 73736 | tf_op jit(solution)/shard_map/ppermute | solution.py:406
  14.5 0.0 collective-permute-done.1.refs_1_
  14.5 2.3 %shard_map.113 = (f32[2,32,128]{2,1,0:T(8,128)S(1)}, f32[2,32,128]{2,1,0:T(8,128)S(1)}, f32[2,32,128]{2,1,0:T(8,128)S(1)}, f32[2,32,128]{2,1,0:T(8,128)S(1)}, f3...) custom-call(bf16[13,13,2,32,128]{4,3,2,1,0:T(8,128)(2,1)} %blocks_hb, ...), custom_call_target="tpu_custom_call" | custom-call | tf_op jit(solution)/shard_map/pallas_call | solution.py:323
  16.8 0.0 collective-permute-done.4.refs_29_
  16.8 0.9 %shard_map.115 = f32[13,2,32,128]{3,2,1,0:T(8,128)} custom-call(f32[2,32,128]{2,1,0:T(8,128)S(1)} %get-tuple-element.104.refs_0_, f32[2,32,128]{2,1,0:T(8,128)S(1)} %get-tuple-element.105.refs_1_, f32[2,32,128]{2,1,0:T(8,128)S(1)} %get-tuple-element.106.refs_2_, f32[2,32,128]{2,1,0:T(8,128)S(1)} %get-tuple-element.107.refs_3_, ...), custom_call_target="tpu_custom_call" | custom-call | tf_op jit(solution)/shard_map/pallas_call | solution.py:323
  (3 shorter events, 0.0 us)
Async XLA Ops:
  1.6 5.4 %collective-permute-start.2 = (f32[6,16,128]{2,1,0:T(8,128)S(1)}, f32[6,16,128]{2,1,0:T(8,128)S(1)}, u32[]{:S(2)}, u32[]{:S(2)}) collective-permute-start(f32[6,16,128]{2,1,0:T(8,128)S(1)} %get-tuple-element.71._.sent_ref.refs_26_), channel_id=1, source_target_pairs={{0,1},{1,0},{2,3},{3,2},{4,5},{5,4},{6,7},{7,6},{8,9},{9,8},{10,11... | collective-permute-start | bytes 147464 | tf_op jit(solution)/shard_map/ppermute | solution.py:406
  7.0 1.8 %collective-permute-start = (f32[56,128]{1,0:T(8,128)S(1)}, f32[56,128]{1,0:T(8,128)S(1)}, u32[]{:S(2)}, u32[]{:S(2)}) collective-permute-start(f32[56,128]{1,0:T(8,128)S(1)} %shard_map.110), channel_id=1, source_target_pairs={{0,8},{8,0},{16,24},{24,16},{1,9},{9,1},{17,25},{25,17},{2,10},{10... | collective-permute-start | bytes 86024 | tf_op jit(solution)/shard_map/ppermute | solution.py:408
  7.1 4.8 %collective-permute-start.3 = (f32[4,16,128]{2,1,0:T(8,128)S(1)}, f32[4,16,128]{2,1,0:T(8,128)S(1)}, u32[]{:S(2)}, u32[]{:S(2)}) collective-permute-start(f32[4,16,128]{2,1,0:T(8,128)S(1)} %get-tuple-element.90.refs_0_.sent_ref), channel_id=1, source_target_pairs={{0,2},{1,3},{2,0},{3,1},{4,6},{5,7},{6,4},{7,5},{8,10},{9,11},{10,... | collective-permute-start | bytes 98312 | tf_op jit(solution)/shard_map/ppermute | solution.py:406
  8.9 5.6 %collective-permute-start.1 = (f32[56,128]{1,0:T(8,128)S(1)}, f32[56,128]{1,0:T(8,128)S(1)}, u32[]{:S(2)}, u32[]{:S(2)}) collective-permute-start(f32[56,128]{1,0:T(8,128)S(1)} %select_add_fusion.refs_1_.sent_ref), channel_id=1, source_target_pairs={{0,24},{8,16},{16,8},{24,0},{1,25},{9,17},{17,9},{25,1},{2,26},{10... | collective-permute-start | bytes 86024 | tf_op jit(solution)/shard_map/ppermute | solution.py:408
  11.9 4.9 %collective-permute-start.4 = (f32[3,16,128]{2,1,0:T(8,128)S(1)}, f32[3,16,128]{2,1,0:T(8,128)S(1)}, u32[]{:S(2)}, u32[]{:S(2)}) collective-permute-start(f32[3,16,128]{2,1,0:T(8,128)S(1)} %get-tuple-element.131), channel_id=1, source_target_pairs={{0,4},{1,5},{2,6},{3,7},{4,0},{5,1},{6,2},{7,3},{8,12},{9,13},{10,... | collective-permute-start | bytes 73736 | tf_op jit(solution)/shard_map/ppermute | solution.py:406

commit v3 on v2

--- a/solution.py
+++ b/solution.py
@@ -263,11 +263,16 @@
                 over = jnp.stack([inc_refs[u][layer - 1] for u in group])
                 total = total + face_refs[2 * layers + layer - 1][...] * (here - over)
             for u in group:
-                flux_ref[u, layer] = total[u - first] + river if u + layer == 0 else total[u - first]
-    for u in range(unknowns):
+                flux_ref[u, layer] = total[u - first]
+    for u in [*range(1, unknowns), 0]:
         total = flux_ref[u]
         if u < count:
-            out_refs[u][...] = total + done_refs[u][...]
+            total = total + done_refs[u][...]
+            if u == 0:
+                out_refs[u][0] = total[0] + river
+                out_refs[u][1:] = total[1:]
+            else:
+                out_refs[u][...] = total
             continue
         at = u - count
         if at % WAITS == 0:

time: 17.9 us -> 17.8 us (level)
  transfers between devices with their start and end apart: 5 -> 5, of which waited for: 0 -> 1; matrix products, arithmetic and copies ran while one was open for 8% -> 9% of each run, Pallas kernels for 24% -> 24%
where the time goes in v3:
time: 17.8 us; the launch traced here: 17.6 us
  starting transfers between devices  8.69 us (49%)
  Pallas kernels  6.64 us (37%)
  other arithmetic  1.5 us (8%)
  between operations  0.72 us (4%)
    ppermute x3, starting transfers between devices, body(): lax.ppermute(y_send, 'ty', [(i, i ^ 1 << k) for i in range(y_size)])  7.44 us
    pallas_call x7, Pallas kernels, call(): pl.pallas_call(kernel, out_shape=[jax.ShapeDtypeStruct(o.shape, o.dtype)...  6.64 us
    ppermute x2, starting transfers between devices, body(): lax.ppermute(x_send, 'tx', [(i, i ^ (2 << k) - 1) for i in range(x_size)])  1.25 us
    select_n x1, other arithmetic, body(): jnp.where(lax.broadcasted_iota(jnp.int32, stored.shape, 2) < reach_local,...  0.72 us
    select_n x1, other arithmetic, body(): jnp.where(live, inflow, 0.0)  0.7 us
  transfers between devices with their start and end apart: 5, of which 1 were waited for; matrix products, arithmetic and copies ran while one was open for 9% of the time, Pallas kernels for 24%

profile of v3, /device:TPU:0, one launch (start us, length us, event | category | flops | bytes accessed | tf_op | source)
XLA Modules:
  0.0 17.6 jit_solution(8928967518203020719)
XLA Ops:
  0.0 1.6 %shard_map.109 = (f32[6,16,128]{2,1,0:T(8,128)S(1)}, f32[32,128]{1,0:T(8,128)S(1)}, f32[2,32,128]{2,1,0:T(8,128)S(1)}, f32[2,32,128]{2,1,0:T(8,128)S(1)}, f32[2,...) custom-call(f32[13,2,32,128]{3,2,1,0:T(8,128)} %inc_hbm.1, ...), custom_call_target="tpu_custom_call" | custom-call | tf_op jit(solution)/shard_map/pallas_call | solution.py:328
  1.6 3.0 %collective-permute-start.2 = (f32[6,16,128]{2,1,0:T(8,128)S(1)}, f32[6,16,128]{2,1,0:T(8,128)S(1)}, u32[]{:S(2)}, u32[]{:S(2)}) collective-permute-start(f32[6,16,128]{2,1,0:T(8,128)S(1)} %get-tuple-element.71._.sent_ref.refs_26_), channel_id=1, source_target_pairs={{0,1},{1,0},{2,3},{3,2},{4,5},{5,4},{6,7},{7,6},{8,9},{9,8},{10,11... | collective-permute-start | bytes 147464 | tf_op jit(solution)/shard_map/ppermute | solution.py:411
  5.2 0.7 %fusion = (f32[1,1,256]{2,1,0:T(1,128)S(1)}, f32[1,1,256]{2,1,0:T(1,128)S(1)}) fusion(f32[1,1,256]{2,1,0:T(1,128)} %param.19, s32[]{:T(128)} %bitcast.4, f32[1,1,256]{2,1,0:T(1,128)} %param.20), kind=kLoop, calls=%fused_computation.5 | loop fusion | flops 768 | bytes 4100 | tf_op jit(solution)/shard_map/jit(_where)/select_n | solution.py:400
  5.9 0.7 %compare_select_fusion = (f32[1,1,256]{2,1,0:T(1,128)S(1)}, f32[1,1,256]{2,1,0:T(1,128)S(1)}) fusion(f32[1,1,64]{2,1,0:T(1,128)} %bitcast.7, s32[]{:T(128)} %bitcast.3, s32[1,1,256]{2,1,0:T(1,128)} %param.16, s32[1,1,256]{2,1,0:T(1,128)} %param.17), kind=kLoop, calls=%fused_computation.1 | loop fusion | flops 2048 | bytes 4356 | tf_op jit(solution)/shard_map/jit(_where)/select_n | solution.py:396
  6.7 0.3 %shard_map.110 = f32[56,128]{1,0:T(8,128)S(1)} custom-call(f32[1,1,256]{2,1,0:T(1,128)S(1)} %get-tuple-element.134.code_ref, f32[1,1,256]{2,1,0:T(1,128)S(1)} %get-tuple-element.136.outflow_ref, f32[1,1,256]{2,1,0:T(1,128)S(1)} %get-tuple-element.135.inflow_ref, f32[1,1,256]{2,1,0:T(1,128)S(1)} %get-tuple-element.133.storage_ref, ...), custom_call_target="tpu_custom_call" | custom-call | tf_op jit(solution)/shard_map/pallas_call | solution.py:328
  7.0 0.0 collective-permute-start
  7.0 0.0 collective-permute-done.2.got_ref.refs_27_
  7.1 1.8 %collective-permute-start.3 = (f32[4,16,128]{2,1,0:T(8,128)S(1)}, f32[4,16,128]{2,1,0:T(8,128)S(1)}, u32[]{:S(2)}, u32[]{:S(2)}) collective-permute-start(f32[4,16,128]{2,1,0:T(8,128)S(1)} %get-tuple-element.90.refs_0_.sent_ref), channel_id=1, source_target_pairs={{0,2},{1,3},{2,0},{3,1},{4,6},{5,7},{6,4},{7,5},{8,10},{9,11},{10,... | collective-permute-start | bytes 98312 | tf_op jit(solution)/shard_map/ppermute | solution.py:411
  8.8 0.0 collective-permute-done.refs_0_
  8.8 0.1 select_add_fusion.refs_1_.sent_ref
  8.9 1.2 %collective-permute-start.1 = (f32[56,128]{1,0:T(8,128)S(1)}, f32[56,128]{1,0:T(8,128)S(1)}, u32[]{:S(2)}, u32[]{:S(2)}) collective-permute-start(f32[56,128]{1,0:T(8,128)S(1)} %select_add_fusion.refs_1_.sent_ref), channel_id=1, source_target_pairs={{0,24},{8,16},{16,8},{24,0},{1,25},{9,17},{17,9},{25,1},{2,26},{10... | collective-permute-start | bytes 86024 | tf_op jit(solution)/shard_map/ppermute | solution.py:413
  10.2 1.7 %shard_map.112 = (f32[2,32,128]{2,1,0:T(8,128)S(1)}, f32[2,32,128]{2,1,0:T(8,128)S(1)}, f32[2,32,128]{2,1,0:T(8,128)S(1)}, f32[2,32,128]{2,1,0:T(8,128)S(1)}, f3...) custom-call(bf16[13,13,2,32,128]{4,3,2,1,0:T(8,128)(2,1)} %blocks_hb, ...), custom_call_target="tpu_custom_call" | custom-call | tf_op jit(solution)/shard_map/pallas_call | solution.py:328
  11.8 0.0 collective-permute-done.3.got_ref.refs_28_
  11.9 2.7 %collective-permute-start.4 = (f32[3,16,128]{2,1,0:T(8,128)S(1)}, f32[3,16,128]{2,1,0:T(8,128)S(1)}, u32[]{:S(2)}, u32[]{:S(2)}) collective-permute-start(f32[3,16,128]{2,1,0:T(8,128)S(1)} %get-tuple-element.131), channel_id=1, source_target_pairs={{0,4},{1,5},{2,6},{3,7},{4,0},{5,1},{6,2},{7,3},{8,12},{9,13},{10,... | collective-permute-start | bytes 73736 | tf_op jit(solution)/shard_map/ppermute | solution.py:411
  14.5 0.0 collective-permute-done.1.refs_1_
  14.5 2.2 %shard_map.113 = (f32[2,32,128]{2,1,0:T(8,128)S(1)}, f32[2,32,128]{2,1,0:T(8,128)S(1)}, f32[2,32,128]{2,1,0:T(8,128)S(1)}, f32[2,32,128]{2,1,0:T(8,128)S(1)}, f3...) custom-call(bf16[13,13,2,32,128]{4,3,2,1,0:T(8,128)(2,1)} %blocks_hb, ...), custom_call_target="tpu_custom_call" | custom-call | tf_op jit(solution)/shard_map/pallas_call | solution.py:328
  16.7 0.1 collective-permute-done.4.refs_29_
  16.8 0.8 %shard_map.115 = f32[13,2,32,128]{3,2,1,0:T(8,128)} custom-call(f32[2,32,128]{2,1,0:T(8,128)S(1)} %get-tuple-element.104.refs_0_, f32[2,32,128]{2,1,0:T(8,128)S(1)} %get-tuple-element.105.refs_1_, f32[2,32,128]{2,1,0:T(8,128)S(1)} %get-tuple-element.106.refs_2_, f32[2,32,128]{2,1,0:T(8,128)S(1)} %get-tuple-element.107.refs_3_, ...), custom_call_target="tpu_custom_call" | custom-call | tf_op jit(solution)/shard_map/pallas_call | solution.py:328
  (3 shorter events, 0.0 us)
Async XLA Ops:
  1.6 5.4 %collective-permute-start.2 = (f32[6,16,128]{2,1,0:T(8,128)S(1)}, f32[6,16,128]{2,1,0:T(8,128)S(1)}, u32[]{:S(2)}, u32[]{:S(2)}) collective-permute-start(f32[6,16,128]{2,1,0:T(8,128)S(1)} %get-tuple-element.71._.sent_ref.refs_26_), channel_id=1, source_target_pairs={{0,1},{1,0},{2,3},{3,2},{4,5},{5,4},{6,7},{7,6},{8,9},{9,8},{10,11... | collective-permute-start | bytes 147464 | tf_op jit(solution)/shard_map/ppermute | solution.py:411
  7.0 1.8 %collective-permute-start = (f32[56,128]{1,0:T(8,128)S(1)}, f32[56,128]{1,0:T(8,128)S(1)}, u32[]{:S(2)}, u32[]{:S(2)}) collective-permute-start(f32[56,128]{1,0:T(8,128)S(1)} %shard_map.110), channel_id=1, source_target_pairs={{0,8},{8,0},{16,24},{24,16},{1,9},{9,1},{17,25},{25,17},{2,10},{10... | collective-permute-start | bytes 86024 | tf_op jit(solution)/shard_map/ppermute | solution.py:413
  7.1 4.8 %collective-permute-start.3 = (f32[4,16,128]{2,1,0:T(8,128)S(1)}, f32[4,16,128]{2,1,0:T(8,128)S(1)}, u32[]{:S(2)}, u32[]{:S(2)}) collective-permute-start(f32[4,16,128]{2,1,0:T(8,128)S(1)} %get-tuple-element.90.refs_0_.sent_ref), channel_id=1, source_target_pairs={{0,2},{1,3},{2,0},{3,1},{4,6},{5,7},{6,4},{7,5},{8,10},{9,11},{10,... | collective-permute-start | bytes 98312 | tf_op jit(solution)/shard_map/ppermute | solution.py:411
  8.9 5.6 %collective-permute-start.1 = (f32[56,128]{1,0:T(8,128)S(1)}, f32[56,128]{1,0:T(8,128)S(1)}, u32[]{:S(2)}, u32[]{:S(2)}) collective-permute-start(f32[56,128]{1,0:T(8,128)S(1)} %select_add_fusion.refs_1_.sent_ref), channel_id=1, source_target_pairs={{0,24},{8,16},{16,8},{24,0},{1,25},{9,17},{17,9},{25,1},{2,26},{10... | collective-permute-start | bytes 86024 | tf_op jit(solution)/shard_map/ppermute | solution.py:413
  11.9 4.9 %collective-permute-start.4 = (f32[3,16,128]{2,1,0:T(8,128)S(1)}, f32[3,16,128]{2,1,0:T(8,128)S(1)}, u32[]{:S(2)}, u32[]{:S(2)}) collective-permute-start(f32[3,16,128]{2,1,0:T(8,128)S(1)} %get-tuple-element.131), channel_id=1, source_target_pairs={{0,4},{1,5},{2,6},{3,7},{4,0},{5,1},{6,2},{7,3},{8,12},{9,13},{10,... | collective-permute-start | bytes 73736 | tf_op jit(solution)/shard_map/ppermute | solution.py:411

commit v4 on v3

--- a/solution.py
+++ b/solution.py
@@ -149,6 +149,11 @@
         if k == 0:
             passed = jnp.where(upper, passed, got_ref[2 + layers + layer])
         send_ref[lead + layer] = passed
+
+
+def sum_kernel(start, stop, sent_ref, got_ref, _, send_ref):
+    send_ref[...] = sent_ref[...]
+    send_ref[start:stop, :] = sent_ref[start:stop, :] + got_ref[start:stop, :]
 
 
 def beside_x(received, rows):
@@ -350,9 +355,9 @@
 RIVER_COST = 0
 GROUP = 13
 WAITS = 2
-AHEAD = 4
+AHEAD = 5
 EXTRA = 0
-AHEAD_GRANT = 54080
+AHEAD_GRANT = 54180
 
 
 def body(
@@ -404,26 +409,23 @@
     y_got = []
     x_got = []
     prior = None
-    at = lax.broadcasted_iota(jnp.int32, x_send.shape, 0)
-    summed = (at >= rows) & (at < rows + 2 * pad)
+    ahead = (y_first,)
     for k in range(max(x_rounds, y_rounds)):
         if k < y_rounds:
             y_got.append(lax.ppermute(y_send, "ty", [(i, i ^ (1 << k)) for i in range(y_size)]))
         if k < x_rounds:
             x_got.append(lax.ppermute(x_send, "tx", [(i, i ^ ((2 << k) - 1)) for i in range(x_size)]))
-            if k + 1 < x_rounds:
-                x_send = x_send + jnp.where(summed, x_got[-1], 0.0)
         if k + 1 < y_rounds:
             y_send, prior = call(
                 functools.partial(between_kernel, k, layers),
                 [f32((2 if k + 2 < y_rounds else 1) + layers, tall, cols), f32(2, tall, cols)],
-                [y_send, y_got[-1]] + ([prior] + list(ahead[:1]) if k > 0 else []),
+                [y_send, y_got[-1]] + ([prior, x_send] if k > 0 else []),
             )
             if k == 0:
                 made = call(
                     functools.partial(ahead_kernel, unknowns, AHEAD),
                     [f32(layers, rows, cols)] * AHEAD + [plane] * (2 * unknowns - AHEAD),
-                    [blocks, decay, y_send, x_send, *kept[:unknowns]],
+                    [blocks, decay, y_send, y_send, *kept[:unknowns]],
                     far=2,
                     scratch=[
                         like(blocks, AHEAD, *blocks.shape[1:]), like(decay), like(decay), like(decay), like(decay),
@@ -432,6 +434,10 @@
                     grant=AHEAD_GRANT,
                 )
                 ahead, grown = made[:unknowns], made[unknowns:]
+        if k + 1 < x_rounds:
+            (x_send,) = call(
+                functools.partial(sum_kernel, rows, rows + 2 * pad), [x_send], [x_send, x_got[-1], ahead[0]]
+            )
     local = call(
         functools.partial(local_kernel, x_rounds, pad, reach_rows, slots, unknowns, layers, AHEAD),
         [f32(layers, rows, cols)] * unknowns,

time: 17.8 us -> 17.8 us (level)
    pallas_call x7 -> x8, Pallas kernels: 6.64 us -> 6.73 us  [call(): pl.pallas_call(kernel, out_shape=[jax.ShapeDtypeStruct(o.shape, o.dtype)...]
  transfers between devices with their start and end apart: 5 -> 5, of which waited for: 1 -> 0; matrix products, arithmetic and copies ran while one was open for 9% -> 8% of each run, Pallas kernels for 24% -> 24%
where the time goes in v4:
time: 17.8 us; the launch traced here: 17.6 us
  starting transfers between devices  8.71 us (49%)
  Pallas kernels  6.73 us (38%)
  other arithmetic  1.42 us (8%)
  between operations  0.72 us (4%)
    ppermute x3, starting transfers between devices, body(): lax.ppermute(y_send, 'ty', [(i, i ^ 1 << k) for i in range(y_size)])  7.45 us
    pallas_call x8, Pallas kernels, call(): pl.pallas_call(kernel, out_shape=[jax.ShapeDtypeStruct(o.shape, o.dtype)...  6.73 us
    ppermute x2, starting transfers between devices, body(): lax.ppermute(x_send, 'tx', [(i, i ^ (2 << k) - 1) for i in range(x_size)])  1.26 us
    select_n x1, other arithmetic, body(): jnp.where(lax.broadcasted_iota(jnp.int32, stored.shape, 2) < reach_local,...  0.72 us
    select_n x1, other arithmetic, body(): jnp.where(live, inflow, 0.0)  0.7 us
  transfers between devices with their start and end apart: 5, of which 0 were waited for; matrix products, arithmetic and copies ran while one was open for 8% of the time, Pallas kernels for 24%

profile of v4, /device:TPU:0, one launch (start us, length us, event | category | flops | bytes accessed | tf_op | source)
XLA Modules:
  0.0 17.6 jit_solution(1663398424557008513)
XLA Ops:
  0.0 1.6 %shard_map.109 = (f32[6,16,128]{2,1,0:T(8,128)S(1)}, f32[32,128]{1,0:T(8,128)S(1)}, f32[2,32,128]{2,1,0:T(8,128)S(1)}, f32[2,32,128]{2,1,0:T(8,128)S(1)}, f32[2,...) custom-call(f32[13,2,32,128]{3,2,1,0:T(8,128)} %inc_hbm.1, ...), custom_call_target="tpu_custom_call" | custom-call | tf_op jit(solution)/shard_map/pallas_call | solution.py:333
  1.6 3.0 %collective-permute-start.1 = (f32[6,16,128]{2,1,0:T(8,128)S(1)}, f32[6,16,128]{2,1,0:T(8,128)S(1)}, u32[]{:S(2)}, u32[]{:S(2)}) collective-permute-start(f32[6,16,128]{2,1,0:T(8,128)S(1)} %get-tuple-element.71._.sent_ref.refs_26_), channel_id=1, source_target_pairs={{0,1},{1,0},{2,3},{3,2},{4,5},{5,4},{6,7},{7,6},{8,9},{9,8},{10,11... | collective-permute-start | bytes 147464 | tf_op jit(solution)/shard_map/ppermute | solution.py:415
  5.2 0.7 %fusion = (f32[1,1,256]{2,1,0:T(1,128)S(1)}, f32[1,1,256]{2,1,0:T(1,128)S(1)}) fusion(f32[1,1,256]{2,1,0:T(1,128)} %param.19, s32[]{:T(128)} %bitcast.4, f32[1,1,256]{2,1,0:T(1,128)} %param.20), kind=kLoop, calls=%fused_computation.3 | loop fusion | flops 768 | bytes 4100 | tf_op jit(solution)/shard_map/jit(_where)/select_n | solution.py:405
  5.9 0.7 %compare_select_fusion = (f32[1,1,256]{2,1,0:T(1,128)S(1)}, f32[1,1,256]{2,1,0:T(1,128)S(1)}) fusion(f32[1,1,64]{2,1,0:T(1,128)} %bitcast.7, s32[]{:T(128)} %bitcast.3, s32[1,1,256]{2,1,0:T(1,128)} %param.16, s32[1,1,256]{2,1,0:T(1,128)} %param.17), kind=kLoop, calls=%fused_computation | loop fusion | flops 2048 | bytes 4356 | tf_op jit(solution)/shard_map/jit(_where)/select_n | solution.py:401
  6.7 0.3 %shard_map.110.sent_ref = f32[56,128]{1,0:T(8,128)S(1)} custom-call(f32[1,1,256]{2,1,0:T(1,128)S(1)} %get-tuple-element.134.code_ref, f32[1,1,256]{2,1,0:T(1,128)S(1)} %get-tuple-element.136.outflow_ref, f32[1,1,256]{2,1,0:T(1,128)S(1)} %get-tuple-element.135.inflow_ref, f32[1,1,256]{2,1,0:T(1,128)S(1)} %get-tuple-element.133.storage_ref, ...), custom_call_target="tpu_custom_call" | custom-call | tf_op jit(solution)/shard_map/pallas_call | solution.py:333
  7.0 0.0 collective-permute-start
  7.0 0.0 collective-permute-done.1.got_ref.refs_27_
  7.1 1.8 %collective-permute-start.3 = (f32[4,16,128]{2,1,0:T(8,128)S(1)}, f32[4,16,128]{2,1,0:T(8,128)S(1)}, u32[]{:S(2)}, u32[]{:S(2)}) collective-permute-start(f32[4,16,128]{2,1,0:T(8,128)S(1)} %get-tuple-element.72.refs_0_.refs_1_.sent_ref), channel_id=1, source_target_pairs={{0,2},{1,3},{2,0},{3,1},{4,6},{5,7},{6,4},{7,5},{8,10},{9,11},{10,... | collective-permute-start | bytes 98312 | tf_op jit(solution)/shard_map/ppermute | solution.py:415
  8.8 1.7 %shard_map.112 = (f32[2,32,128]{2,1,0:T(8,128)S(1)}, f32[2,32,128]{2,1,0:T(8,128)S(1)}, f32[2,32,128]{2,1,0:T(8,128)S(1)}, f32[2,32,128]{2,1,0:T(8,128)S(1)}, f3...) custom-call(bf16[13,13,2,32,128]{4,3,2,1,0:T(8,128)(2,1)} %blocks_hb, ...), custom_call_target="tpu_custom_call" | custom-call | tf_op jit(solution)/shard_map/pallas_call | solution.py:333
  10.6 0.0 collective-permute-done.got_ref.refs_0_
  10.6 1.3 %collective-permute-start.2 = (f32[56,128]{1,0:T(8,128)S(1)}, f32[56,128]{1,0:T(8,128)S(1)}, u32[]{:S(2)}, u32[]{:S(2)}) collective-permute-start(f32[56,128]{1,0:T(8,128)S(1)} %shard_map.113.sent_ref.refs_1_), channel_id=1, source_target_pairs={{0,24},{8,16},{16,8},{24,0},{1,25},{9,17},{17,9},{25,1},{2,26},{10... | collective-permute-start | bytes 86024 | tf_op jit(solution)/shard_map/ppermute | solution.py:417
  11.9 0.0 collective-permute-done.3.got_ref.refs_28_
  11.9 2.7 %collective-permute-start.4 = (f32[3,16,128]{2,1,0:T(8,128)S(1)}, f32[3,16,128]{2,1,0:T(8,128)S(1)}, u32[]{:S(2)}, u32[]{:S(2)}) collective-permute-start(f32[3,16,128]{2,1,0:T(8,128)S(1)} %get-tuple-element.131), channel_id=1, source_target_pairs={{0,4},{1,5},{2,6},{3,7},{4,0},{5,1},{6,2},{7,3},{8,12},{9,13},{10,... | collective-permute-start | bytes 73736 | tf_op jit(solution)/shard_map/ppermute | solution.py:415
  14.5 0.0 collective-permute-done.2.refs_1_
  14.5 2.2 %shard_map.114 = (f32[2,32,128]{2,1,0:T(8,128)S(1)}, f32[2,32,128]{2,1,0:T(8,128)S(1)}, f32[2,32,128]{2,1,0:T(8,128)S(1)}, f32[2,32,128]{2,1,0:T(8,128)S(1)}, f3...) custom-call(bf16[13,13,2,32,128]{4,3,2,1,0:T(8,128)(2,1)} %blocks_hb, ...), custom_call_target="tpu_custom_call" | custom-call | tf_op jit(solution)/shard_map/pallas_call | solution.py:333
  16.7 0.0 collective-permute-done.4.refs_29_
  16.7 0.9 %shard_map.116 = f32[13,2,32,128]{3,2,1,0:T(8,128)} custom-call(f32[2,32,128]{2,1,0:T(8,128)S(1)} %get-tuple-element.104.refs_0_, f32[2,32,128]{2,1,0:T(8,128)S(1)} %get-tuple-element.105.refs_1_, f32[2,32,128]{2,1,0:T(8,128)S(1)} %get-tuple-element.106.refs_2_, f32[2,32,128]{2,1,0:T(8,128)S(1)} %get-tuple-element.107.refs_3_, ...), custom_call_target="tpu_custom_call" | custom-call | tf_op jit(solution)/shard_map/pallas_call | solution.py:333
  (3 shorter events, 0.0 us)
Async XLA Ops:
  1.6 5.4 %collective-permute-start.1 = (f32[6,16,128]{2,1,0:T(8,128)S(1)}, f32[6,16,128]{2,1,0:T(8,128)S(1)}, u32[]{:S(2)}, u32[]{:S(2)}) collective-permute-start(f32[6,16,128]{2,1,0:T(8,128)S(1)} %get-tuple-element.71._.sent_ref.refs_26_), channel_id=1, source_target_pairs={{0,1},{1,0},{2,3},{3,2},{4,5},{5,4},{6,7},{7,6},{8,9},{9,8},{10,11... | collective-permute-start | bytes 147464 | tf_op jit(solution)/shard_map/ppermute | solution.py:415
  7.0 3.6 %collective-permute-start = (f32[56,128]{1,0:T(8,128)S(1)}, f32[56,128]{1,0:T(8,128)S(1)}, u32[]{:S(2)}, u32[]{:S(2)}) collective-permute-start(f32[56,128]{1,0:T(8,128)S(1)} %shard_map.110.sent_ref), channel_id=1, source_target_pairs={{0,8},{8,0},{16,24},{24,16},{1,9},{9,1},{17,25},{25,17},{2,10},{10... | collective-permute-start | bytes 86024 | tf_op jit(solution)/shard_map/ppermute | solution.py:417
  7.1 4.8 %collective-permute-start.3 = (f32[4,16,128]{2,1,0:T(8,128)S(1)}, f32[4,16,128]{2,1,0:T(8,128)S(1)}, u32[]{:S(2)}, u32[]{:S(2)}) collective-permute-start(f32[4,16,128]{2,1,0:T(8,128)S(1)} %get-tuple-element.72.refs_0_.refs_1_.sent_ref), channel_id=1, source_target_pairs={{0,2},{1,3},{2,0},{3,1},{4,6},{5,7},{6,4},{7,5},{8,10},{9,11},{10,... | collective-permute-start | bytes 98312 | tf_op jit(solution)/shard_map/ppermute | solution.py:415
  10.6 3.9 %collective-permute-start.2 = (f32[56,128]{1,0:T(8,128)S(1)}, f32[56,128]{1,0:T(8,128)S(1)}, u32[]{:S(2)}, u32[]{:S(2)}) collective-permute-start(f32[56,128]{1,0:T(8,128)S(1)} %shard_map.113.sent_ref.refs_1_), channel_id=1, source_target_pairs={{0,24},{8,16},{16,8},{24,0},{1,25},{9,17},{17,9},{25,1},{2,26},{10... | collective-permute-start | bytes 86024 | tf_op jit(solution)/shard_map/ppermute | solution.py:417
  11.9 4.9 %collective-permute-start.4 = (f32[3,16,128]{2,1,0:T(8,128)S(1)}, f32[3,16,128]{2,1,0:T(8,128)S(1)}, u32[]{:S(2)}, u32[]{:S(2)}) collective-permute-start(f32[3,16,128]{2,1,0:T(8,128)S(1)} %get-tuple-element.131), channel_id=1, source_target_pairs={{0,4},{1,5},{2,6},{3,7},{4,0},{5,1},{6,2},{7,3},{8,12},{9,13},{10,... | collective-permute-start | bytes 73736 | tf_op jit(solution)/shard_map/ppermute | solution.py:415

commit v5 on v4

--- a/solution.py
+++ b/solution.py
@@ -354,8 +354,8 @@
 LOCAL_COST = 0
 RIVER_COST = 0
 GROUP = 13
-WAITS = 2
-AHEAD = 5
+WAITS = 3
+AHEAD = 3
 EXTRA = 0
 AHEAD_GRANT = 54180
 

time: 17.8 us -> 17.8 us (level)
  no operation moved by 1% of the time
where the time goes in v5:
time: 17.8 us; the launch traced here: 17.6 us
  starting transfers between devices  8.71 us (49%)
  Pallas kernels  6.73 us (38%)
  other arithmetic  1.42 us (8%)
  between operations  0.72 us (4%)
    ppermute x3, starting transfers between devices, body(): lax.ppermute(y_send, 'ty', [(i, i ^ 1 << k) for i in range(y_size)])  7.45 us
    pallas_call x8, Pallas kernels, call(): pl.pallas_call(kernel, out_shape=[jax.ShapeDtypeStruct(o.shape, o.dtype)...  6.73 us
    ppermute x2, starting transfers between devices, body(): lax.ppermute(x_send, 'tx', [(i, i ^ (2 << k) - 1) for i in range(x_size)])  1.26 us
    select_n x1, other arithmetic, body(): jnp.where(lax.broadcasted_iota(jnp.int32, stored.shape, 2) < reach_local,...  0.72 us
    select_n x1, other arithmetic, body(): jnp.where(live, inflow, 0.0)  0.7 us
  transfers between devices with their start and end apart: 5, of which 0 were waited for; matrix products, arithmetic and copies ran while one was open for 8% of the time, Pallas kernels for 24%

profile of v5, /device:TPU:0, one launch (start us, length us, event | category | flops | bytes accessed | tf_op | source)
XLA Modules:
  0.0 17.6 jit_solution(16794981143639742655)
XLA Ops:
  0.0 1.6 %shard_map.109 = (f32[6,16,128]{2,1,0:T(8,128)S(1)}, f32[32,128]{1,0:T(8,128)S(1)}, f32[2,32,128]{2,1,0:T(8,128)S(1)}, f32[2,32,128]{2,1,0:T(8,128)S(1)}, f32[2,...) custom-call(f32[13,2,32,128]{3,2,1,0:T(8,128)} %inc_hbm.1, ...), custom_call_target="tpu_custom_call" | custom-call | tf_op jit(solution)/shard_map/pallas_call | solution.py:333
  1.6 3.0 %collective-permute-start.1 = (f32[6,16,128]{2,1,0:T(8,128)S(1)}, f32[6,16,128]{2,1,0:T(8,128)S(1)}, u32[]{:S(2)}, u32[]{:S(2)}) collective-permute-start(f32[6,16,128]{2,1,0:T(8,128)S(1)} %get-tuple-element.71._.sent_ref.refs_26_), channel_id=1, source_target_pairs={{0,1},{1,0},{2,3},{3,2},{4,5},{5,4},{6,7},{7,6},{8,9},{9,8},{10,11... | collective-permute-start | bytes 147464 | tf_op jit(solution)/shard_map/ppermute | solution.py:415
  5.2 0.7 %fusion = (f32[1,1,256]{2,1,0:T(1,128)S(1)}, f32[1,1,256]{2,1,0:T(1,128)S(1)}) fusion(f32[1,1,256]{2,1,0:T(1,128)} %param.19, s32[]{:T(128)} %bitcast.4, f32[1,1,256]{2,1,0:T(1,128)} %param.20), kind=kLoop, calls=%fused_computation.3 | loop fusion | flops 768 | bytes 4100 | tf_op jit(solution)/shard_map/jit(_where)/select_n | solution.py:405
  5.9 0.7 %compare_select_fusion = (f32[1,1,256]{2,1,0:T(1,128)S(1)}, f32[1,1,256]{2,1,0:T(1,128)S(1)}) fusion(f32[1,1,64]{2,1,0:T(1,128)} %bitcast.7, s32[]{:T(128)} %bitcast.3, s32[1,1,256]{2,1,0:T(1,128)} %param.16, s32[1,1,256]{2,1,0:T(1,128)} %param.17), kind=kLoop, calls=%fused_computation | loop fusion | flops 2048 | bytes 4356 | tf_op jit(solution)/shard_map/jit(_where)/select_n | solution.py:401
  6.7 0.3 %shard_map.110.sent_ref = f32[56,128]{1,0:T(8,128)S(1)} custom-call(f32[1,1,256]{2,1,0:T(1,128)S(1)} %get-tuple-element.134.code_ref, f32[1,1,256]{2,1,0:T(1,128)S(1)} %get-tuple-element.136.outflow_ref, f32[1,1,256]{2,1,0:T(1,128)S(1)} %get-tuple-element.135.inflow_ref, f32[1,1,256]{2,1,0:T(1,128)S(1)} %get-tuple-element.133.storage_ref, ...), custom_call_target="tpu_custom_call" | custom-call | tf_op jit(solution)/shard_map/pallas_call | solution.py:333
  7.0 0.0 collective-permute-start
  7.0 0.0 collective-permute-done.1.got_ref.refs_27_
  7.1 1.8 %collective-permute-start.3 = (f32[4,16,128]{2,1,0:T(8,128)S(1)}, f32[4,16,128]{2,1,0:T(8,128)S(1)}, u32[]{:S(2)}, u32[]{:S(2)}) collective-permute-start(f32[4,16,128]{2,1,0:T(8,128)S(1)} %get-tuple-element.72.refs_0_.refs_1_.sent_ref), channel_id=1, source_target_pairs={{0,2},{1,3},{2,0},{3,1},{4,6},{5,7},{6,4},{7,5},{8,10},{9,11},{10,... | collective-permute-start | bytes 98312 | tf_op jit(solution)/shard_map/ppermute | solution.py:415
  8.8 1.6 %shard_map.112 = (f32[2,32,128]{2,1,0:T(8,128)S(1)}, f32[2,32,128]{2,1,0:T(8,128)S(1)}, f32[2,32,128]{2,1,0:T(8,128)S(1)}, f32[32,128]{1,0:T(8,128)S(1)}, f32[32...) custom-call(bf16[13,13,2,32,128]{4,3,2,1,0:T(8,128)(2,1)} %blocks_hb, ...), custom_call_target="tpu_custom_call" | custom-call | tf_op jit(solution)/shard_map/pallas_call | solution.py:333
  10.5 0.0 collective-permute-done.got_ref.refs_0_
  10.5 1.3 %collective-permute-start.2 = (f32[56,128]{1,0:T(8,128)S(1)}, f32[56,128]{1,0:T(8,128)S(1)}, u32[]{:S(2)}, u32[]{:S(2)}) collective-permute-start(f32[56,128]{1,0:T(8,128)S(1)} %shard_map.113.sent_ref.refs_1_), channel_id=1, source_target_pairs={{0,24},{8,16},{16,8},{24,0},{1,25},{9,17},{17,9},{25,1},{2,26},{10... | collective-permute-start | bytes 86024 | tf_op jit(solution)/shard_map/ppermute | solution.py:417
  11.7 0.0 collective-permute-done.3.got_ref.refs_28_
  11.7 2.7 %collective-permute-start.4 = (f32[3,16,128]{2,1,0:T(8,128)S(1)}, f32[3,16,128]{2,1,0:T(8,128)S(1)}, u32[]{:S(2)}, u32[]{:S(2)}) collective-permute-start(f32[3,16,128]{2,1,0:T(8,128)S(1)} %get-tuple-element.131), channel_id=1, source_target_pairs={{0,4},{1,5},{2,6},{3,7},{4,0},{5,1},{6,2},{7,3},{8,12},{9,13},{10,... | collective-permute-start | bytes 73736 | tf_op jit(solution)/shard_map/ppermute | solution.py:415
  14.4 0.0 collective-permute-done.2.refs_1_
  14.4 2.3 %shard_map.114 = (f32[2,32,128]{2,1,0:T(8,128)S(1)}, f32[2,32,128]{2,1,0:T(8,128)S(1)}, f32[2,32,128]{2,1,0:T(8,128)S(1)}, f32[2,32,128]{2,1,0:T(8,128)S(1)}, f3...) custom-call(bf16[13,13,2,32,128]{4,3,2,1,0:T(8,128)(2,1)} %blocks_hb, ...), custom_call_target="tpu_custom_call" | custom-call | tf_op jit(solution)/shard_map/pallas_call | solution.py:333
  16.7 0.0 collective-permute-done.4.refs_29_
  16.7 0.9 %shard_map.116 = f32[13,2,32,128]{3,2,1,0:T(8,128)} custom-call(f32[2,32,128]{2,1,0:T(8,128)S(1)} %get-tuple-element.104.refs_0_, f32[2,32,128]{2,1,0:T(8,128)S(1)} %get-tuple-element.105.refs_1_, f32[2,32,128]{2,1,0:T(8,128)S(1)} %get-tuple-element.106.refs_2_, f32[2,32,128]{2,1,0:T(8,128)S(1)} %get-tuple-element.107.refs_3_, ...), custom_call_target="tpu_custom_call" | custom-call | tf_op jit(solution)/shard_map/pallas_call | solution.py:333
  (3 shorter events, 0.0 us)
Async XLA Ops:
  1.6 5.4 %collective-permute-start.1 = (f32[6,16,128]{2,1,0:T(8,128)S(1)}, f32[6,16,128]{2,1,0:T(8,128)S(1)}, u32[]{:S(2)}, u32[]{:S(2)}) collective-permute-start(f32[6,16,128]{2,1,0:T(8,128)S(1)} %get-tuple-element.71._.sent_ref.refs_26_), channel_id=1, source_target_pairs={{0,1},{1,0},{2,3},{3,2},{4,5},{5,4},{6,7},{7,6},{8,9},{9,8},{10,11... | collective-permute-start | bytes 147464 | tf_op jit(solution)/shard_map/ppermute | solution.py:415
  7.0 3.4 %collective-permute-start = (f32[56,128]{1,0:T(8,128)S(1)}, f32[56,128]{1,0:T(8,128)S(1)}, u32[]{:S(2)}, u32[]{:S(2)}) collective-permute-start(f32[56,128]{1,0:T(8,128)S(1)} %shard_map.110.sent_ref), channel_id=1, source_target_pairs={{0,8},{8,0},{16,24},{24,16},{1,9},{9,1},{17,25},{25,17},{2,10},{10... | collective-permute-start | bytes 86024 | tf_op jit(solution)/shard_map/ppermute | solution.py:417
  7.1 4.7 %collective-permute-start.3 = (f32[4,16,128]{2,1,0:T(8,128)S(1)}, f32[4,16,128]{2,1,0:T(8,128)S(1)}, u32[]{:S(2)}, u32[]{:S(2)}) collective-permute-start(f32[4,16,128]{2,1,0:T(8,128)S(1)} %get-tuple-element.72.refs_0_.refs_1_.sent_ref), channel_id=1, source_target_pairs={{0,2},{1,3},{2,0},{3,1},{4,6},{5,7},{6,4},{7,5},{8,10},{9,11},{10,... | collective-permute-start | bytes 98312 | tf_op jit(solution)/shard_map/ppermute | solution.py:415
  10.5 3.9 %collective-permute-start.2 = (f32[56,128]{1,0:T(8,128)S(1)}, f32[56,128]{1,0:T(8,128)S(1)}, u32[]{:S(2)}, u32[]{:S(2)}) collective-permute-start(f32[56,128]{1,0:T(8,128)S(1)} %shard_map.113.sent_ref.refs_1_), channel_id=1, source_target_pairs={{0,24},{8,16},{16,8},{24,0},{1,25},{9,17},{17,9},{25,1},{2,26},{10... | collective-permute-start | bytes 86024 | tf_op jit(solution)/shard_map/ppermute | solution.py:417
  11.7 5.0 %collective-permute-start.4 = (f32[3,16,128]{2,1,0:T(8,128)S(1)}, f32[3,16,128]{2,1,0:T(8,128)S(1)}, u32[]{:S(2)}, u32[]{:S(2)}) collective-permute-start(f32[3,16,128]{2,1,0:T(8,128)S(1)} %get-tuple-element.131), channel_id=1, source_target_pairs={{0,4},{1,5},{2,6},{3,7},{4,0},{5,1},{6,2},{7,3},{8,12},{9,13},{10,... | collective-permute-start | bytes 73736 | tf_op jit(solution)/shard_map/ppermute | solution.py:415
